TPU v7x, 32 devices: a whole 2x2x4 slice. The times are simulated.
32 devices in a mesh: lat: 8 (over z, y), lon: 4 (over x, core).
Axes of the slice: x: 2, y: 2, z: 4, core: 2. Of those that a mesh axis runs over, the one named last changes fastest.
Arguments:
- tokens: bfloat16 [2, 96, 192, 512], P(None, 'lat', 'lon'), may hold values from -12 to 12
- gains: float32 [4, 512], replicated, may hold values from 0.1 to 1.9
- w_qkv: bfloat16 [2, 512, 1536], replicated, may hold values from -10 to 10
- w_proj: bfloat16 [2, 512, 512], replicated, may hold values from -0.25 to 0.25
- w_in: bfloat16 [2, 512, 1024], replicated, may hold values from -0.25 to 0.25
- w_out: bfloat16 [2, 1024, 512], replicated, may hold values from -0.1875 to 0.1875
Outputs:
- evolved: bfloat16 [2, 96, 192, 512], P(None, 'lat', 'lon')
All inputs are finite; a program needn't handle non-finite values.
Results may differ from a plain program's by a relative error of at most 0.013.
The roundings to bfloat16 on the way count: a program that leaves them out, or rounds other values in their place, can miss the bound.
Values may be sent and summed in bfloat16 or wider, within the bound.
No kernel may reach another device: no remote copies, remote signals or barrier semaphores. Data moves between devices by JAX's collectives and lax.ppermute only.
A program may use at most 128 MiB of HBM per device.

v0:
```python
import jax
import jax.numpy as jnp
import numpy as np
from jax import lax
from jax.experimental import pallas as pl
from jax.experimental.pallas import tpu as pltpu
from jax.sharding import PartitionSpec as P

HEADS = 16
WY = 12
WX = 6
SY = 6
SX = 3
EPSILON = 1e-05
NEGATIVE = -1e30
BF = jnp.bfloat16
F32 = jnp.float32
GROUP = 4
EXP_SCALE = float(32.0 ** -0.5 * np.log2(np.e))


def norm(values, gain_row):
    centered = values - jnp.mean(values, axis=-1, keepdims=True)
    variance = jnp.mean(centered * centered, axis=-1, keepdims=True)
    return (centered * lax.rsqrt(variance + EPSILON) * gain_row).astype(BF)


def dot(a, b):
    return jnp.dot(a, b, preferred_element_type=F32)


def attend(q, k, v, bias):
    n, channels = q.shape
    head = channels // HEADS
    lane = lax.broadcasted_iota(jnp.int32, (1, 128), 1) // head
    lanes = lax.broadcasted_iota(jnp.int32, (n, 128), 1) // head
    pieces = []
    for g in range(channels // 128):
        cut = slice(128 * g, 128 * g + 128)
        qg = q[:, cut]
        stacked = jnp.concatenate(
            [qg * (lane == j).astype(F32) for j in range(GROUP)], axis=0
        ).astype(BF)
        s = lax.dot_general(
            stacked, k[:, cut], (((1,), (1,)), ((), ())), preferred_element_type=F32
        )
        if bias is not None:
            s = s + jnp.concatenate([bias] * GROUP, axis=0)
        p = jnp.exp2((s - jnp.max(s, axis=-1, keepdims=True)) * EXP_SCALE)
        w = (p * (1.0 / jnp.sum(p, axis=-1, keepdims=True))).astype(BF)
        o = dot(w, v[:, cut])
        total = o[:n]
        for j in range(1, GROUP):
            total = jnp.where(lanes == j, o[j * n : (j + 1) * n], total)
        pieces.append(total)
    return jnp.concatenate(pieces, axis=1)


def finish(x, attended, gain_row, w_proj, w_in, w_out):
    mixed = (x.astype(F32) + dot(attended, w_proj)).astype(BF)
    normed = norm(mixed.astype(F32), gain_row)
    h = dot(normed, w_in)
    h = jax.nn.gelu(h, approximate=True).astype(BF)
    return mixed.astype(F32) + dot(h, w_out)


def block0(x_ref, perm_ref, gains_ref, wqkv_ref, wproj_ref, win_ref, wout_ref,
           x1_ref, n1_ref, xs, qkv, att, xf):
    tokens, channels = xs.shape
    half = tokens // 2
    strips = half // 72
    quarter = half // 2
    perm = perm_ref[...]
    parts = []
    for r in range(2):
        nat = jnp.concatenate([x_ref[z, quarter * r : quarter * (r + 1)] for z in range(2)], axis=0)
        parts.append(dot(perm, nat).reshape(strips, 72, channels))
    x = jnp.concatenate(parts, axis=1).reshape(tokens, channels)
    xs[...] = x.astype(BF)
    rows = 2 * 144
    steps = tokens // rows

    def project(i, _):
        at = pl.ds(pl.multiple_of(i * rows, 16), rows)
        normed = norm(xs[at].astype(F32), gains_ref[0:1])
        qkv[at] = dot(normed, wqkv_ref[0]).astype(BF)
        return 0

    lax.fori_loop(0, steps, project, 0)

    def window(i, _):
        at = pl.ds(pl.multiple_of(i * 144, 16), 144)
        q = qkv[at, :channels].astype(F32)
        att[at] = attend(q, qkv[at, channels : 2 * channels], qkv[at, 2 * channels :], None).astype(BF)
        return 0

    lax.fori_loop(0, strips, window, 0)

    def close(i, _):
        at = pl.ds(pl.multiple_of(i * rows, 16), rows)
        xf[at] = finish(xs[at], att[at], gains_ref[1:2], wproj_ref[0], win_ref[0], wout_ref[0])
        return 0

    lax.fori_loop(0, steps, close, 0)
    for r in range(2):
        mine = xf[...].reshape(strips, 2, 72, channels)[:, r].reshape(half, channels)
        mine = pltpu.roll(mine, 36, 0).astype(BF)
        x1_ref[r] = mine
        n1_ref[r] = norm(mine.astype(F32), gains_ref[2:3])


def block1(x_ref, n_ref, top_ref, bot_ref, left_ref, right_ref, tl_ref, tr_ref, bl_ref, br_ref,
           bias_ref, perm_ref, gains_ref, wqkv_ref, wproj_ref, win_ref, wout_ref,
           out_ref, lhs, qs, kv, os, done):
    _, half, channels = x_ref.shape
    strips = half // 72
    wins = strips + 1
    first = lax.broadcasted_iota(jnp.int32, (72, channels), 0) < 36
    quarter = half // 2
    sides = (
        (top_ref, tl_ref, tr_ref),
        (bot_ref, bl_ref, br_ref),
    )

    def extend(own, left, right):
        own = own.astype(F32).reshape(strips, 72, channels)
        lead = jnp.where(first, left.astype(F32), own[0])
        tail = jnp.where(first, own[0], right.astype(F32))
        return jnp.concatenate([lead[None], own[1:], tail[None]], axis=0)

    for r in range(2):
        own = extend(n_ref[r], left_ref[r], right_ref[r])
        far_ref, fl_ref, fr_ref = sides[r]
        far = extend(far_ref[...], fl_ref[...], fr_ref[...])
        both = jnp.concatenate([own, far], axis=1).reshape(wins * 144, channels)
        lhs[...] = both.astype(BF)
        q = dot(own.reshape(wins * 72, channels).astype(BF), wqkv_ref[0, :, :channels])
        qs[...] = q.astype(BF).astype(F32).reshape(wins, 72, channels)
        rows = 3 * 144

        def project(i, _):
            at = pl.ds(pl.multiple_of(i * rows, 16), rows)
            kv[at] = dot(lhs[at], wqkv_ref[0, :, channels:]).astype(BF)
            return 0

        lax.fori_loop(0, wins * 144 // rows, project, 0)

        def window(i, _):
            at = pl.ds(pl.multiple_of(i * 144, 16), 144)
            os[i] = attend(qs[i], kv[at, :channels], kv[at, channels:], bias_ref[r])
            return 0

        lax.fori_loop(0, wins, window, 0)
        edge = jnp.where(first, os[wins - 1], os[0])
        attended = jnp.concatenate([edge[None], os[1:strips]], axis=0).reshape(half, channels).astype(BF)
        for i in range(2):
            at = slice(i * quarter, (i + 1) * quarter)
            done[at] = finish(
                x_ref[r, at], attended[at], gains_ref[3:4], wproj_ref[0], win_ref[0], wout_ref[0]
            ).astype(BF)
        nat = dot(perm_ref[...], done[...]).astype(BF)
        for z in range(2):
            out_ref[z, quarter * r : quarter * (r + 1)] = nat[quarter * z : quarter * (z + 1)]


def orders(strips):
    unit, lev, row, col = np.meshgrid(
        np.arange(2 * strips), np.arange(2), np.arange(SY), np.arange(SX), indexing="ij"
    )
    breadth = WX * strips
    return (lev * SY * breadth + row * breadth + unit * SX + col).reshape(-1)


def whole(shape):
    return pl.BlockSpec(shape, lambda i, n=len(shape): (0,) * n)


def layer(shape, index):
    return pl.BlockSpec((1,) + shape[1:], lambda i: (index, 0, 0))


def shards(tokens, gains, w_qkv, w_proj, w_in, w_out):
    levels, height, breadth, channels = tokens.shape
    half = levels * SY * breadth
    strips = breadth // WX
    order = orders(strips)
    onehot = np.zeros((half, half), np.float32)
    onehot[np.arange(half), order] = 1.0
    back = np.roll(onehot, 36, axis=0).T
    params = pltpu.CompilerParams(
        dimension_semantics=("arbitrary",), vmem_limit_bytes=56 * 1024 * 1024
    )
    weights = (w_qkv, w_proj, w_in, w_out)
    tile = (2, half, channels)
    x1, n1 = pl.pallas_call(
        block0,
        grid=(1,),
        in_specs=[whole((2, half, channels)), whole((half, half)), whole(gains.shape)]
        + [layer(w.shape, 0) for w in weights],
        out_specs=[whole(tile), whole(tile)],
        out_shape=[jax.ShapeDtypeStruct(tile, BF)] * 2,
        scratch_shapes=[
            pltpu.VMEM((2 * half, channels), BF),
            pltpu.VMEM((2 * half, 3 * channels), BF),
            pltpu.VMEM((2 * half, channels), BF),
            pltpu.VMEM((2 * half, channels), F32),
        ],
        compiler_params=params,
        name="regular",
    )(tokens.reshape(2, half, channels), jnp.asarray(onehot, BF), gains, *weights)

    lats, lons = lax.axis_size("lat"), lax.axis_size("lon")

    def move(block, dlat, dlon):
        route = [
            ((y + dlat) * lons + (x + dlon) % lons, y * lons + x)
            for y in range(lats)
            for x in range(lons)
            if 0 <= y + dlat < lats
        ]
        return lax.ppermute(block, ("lat", "lon"), route)

    bot = move(n1[0], 1, 0)
    top = move(n1[1], -1, 0)
    edge = n1[:, :72]
    left, right = move(edge, 0, -1), move(edge, 0, 1)
    tl, tr = move(edge[1], -1, -1), move(edge[1], -1, 1)
    bl, br = move(edge[0], 1, -1), move(edge[0], 1, 1)

    place = lax.axis_index("lat")
    token = np.arange(72)
    lev = token % 36 // 18
    same = np.tile(lev[:, None] == lev[None, :], (1, 2))
    far = np.arange(144) >= 72
    dead = jnp.stack([place == 0, place == lats - 1])
    allowed = same[None] & ~(dead[:, None, None] & far[None, None, :])
    bias = jnp.where(allowed, 0.0, NEGATIVE).astype(F32)
    wins = strips + 1
    out = pl.pallas_call(
        block1,
        grid=(1,),
        in_specs=[whole(a.shape) for a in (x1, n1, top, bot, left, right, tl, tr, bl, br, bias)]
        + [whole((half, half)), whole(gains.shape)]
        + [layer(w.shape, 1) for w in weights],
        out_specs=whole(tile),
        out_shape=jax.ShapeDtypeStruct(tile, BF),
        scratch_shapes=[
            pltpu.VMEM((wins * 144, channels), BF),
            pltpu.VMEM((wins, 72, channels), F32),
            pltpu.VMEM((wins * 144, 2 * channels), BF),
            pltpu.VMEM((wins, 72, channels), F32),
            pltpu.VMEM((half, channels), BF),
        ],
        compiler_params=params,
        name="shifted",
    )(x1, n1, top, bot, left, right, tl, tr, bl, br, bias, jnp.asarray(back, BF), gains, *weights)
    return out.reshape(tokens.shape)


def solution(mesh):
    in_specs = (P(None, "lat", "lon", None), P(), P(), P(), P(), P())
    out_specs = P(None, "lat", "lon", None)
    return jax.shard_map(shards, mesh=mesh, in_specs=in_specs, out_specs=out_specs, check_vma=False)
```

profile of v0, /device:TPU:13, one launch (start us, length us, event | category | flops | bytes accessed | tf_op | source)
XLA Modules:
  0.0 111.8 jit_solution(3034930032419808383)
XLA Ops:
  0.0 28.2 %regular.1 = (bf16[2,576,512]{2,1,0:T(8,128)(2,1)}, bf16[2,576,512]{2,1,0:T(8,128)(2,1)}) custom-call(bf16[2,576,512]{2,1,0:T(8,128)(2,1)} %bitcast.12, bf16[576,576]{1,0:T(8,128)(2,1)} %constant.22.clone.perm_ref, f32[4,512]{1,0:T(4,128)} %gains_ref.3, bf16[2,512,1536]{2,1,0:T(8,128)(2,1)} %wqkv_ref.3, bf16[2,512,512]{2,1,0:T(8,128)(2,1)} %wproj_ref.3, ...), custom_call_target="tpu_custom_call" | custom-call | tf_op jit(solution)/shard_map/regular/pallas_call | solution.py:195
  28.2 1.3 %slice_bitcast_fusion = (bf16[576,512]{1,0:T(8,128)(2,1)S(1)}, bf16[576,512]{1,0:T(8,128)(2,1)S(1)}) fusion(bf16[2,576,512]{2,1,0:T(8,128)(2,1)} %get-tuple-element.8.n_ref), kind=kLoop, calls=%fused_computation | loop fusion | bytes 2359296 | tf_op jit(solution)/shard_map/squeeze | solution.py:223
  29.6 2.1 %collective-permute-start.1 = (bf16[576,512]{1,0:T(8,128)(2,1)S(1)}, bf16[576,512]{1,0:T(8,128)(2,1)S(1)}, u32[]{:S(2)}, u32[]{:S(2)}) collective-permute-start(bf16[576,512]{1,0:T(8,128)(2,1)S(1)} %get-tuple-element.11), channel_id=1, source_target_pairs={{4,0},{5,1},{6,2},{7,3},{8,4},{9,5},{10,6},{11,7},{12,8},{13,9},{1... | collective-permute-start | bytes 1769480 | tf_op jit(solution)/shard_map/ppermute | solution.py:221
  31.7 4.1 %collective-permute-start = (bf16[576,512]{1,0:T(8,128)(2,1)S(1)}, bf16[576,512]{1,0:T(8,128)(2,1)S(1)}, u32[]{:S(2)}, u32[]{:S(2)}) collective-permute-start(bf16[576,512]{1,0:T(8,128)(2,1)S(1)} %get-tuple-element.12), channel_id=1, source_target_pairs={{0,4},{1,5},{2,6},{3,7},{4,8},{5,9},{6,10},{7,11},{8,12},{9,13},{1... | collective-permute-start | bytes 1769480 | tf_op jit(solution)/shard_map/ppermute | solution.py:221
  35.8 0.9 slice_bitcast_fusion.2
  36.7 2.4 %collective-permute-start.7 = (bf16[72,512]{1,0:T(8,128)(2,1)S(1)}, bf16[72,512]{1,0:T(8,128)(2,1)S(1)}, u32[]{:S(2)}, u32[]{:S(2)}) collective-permute-start(bf16[72,512]{1,0:T(8,128)(2,1)S(1)} %get-tuple-element.9), channel_id=1, source_target_pairs={{5,0},{6,1},{7,2},{4,3},{9,4},{10,5},{11,6},{8,7},{13,8},{14,9},{1... | collective-permute-start | bytes 221192 | tf_op jit(solution)/shard_map/ppermute | solution.py:221
  39.1 4.0 %collective-permute-start.6 = (bf16[72,512]{1,0:T(8,128)(2,1)S(1)}, bf16[72,512]{1,0:T(8,128)(2,1)S(1)}, u32[]{:S(2)}, u32[]{:S(2)}) collective-permute-start(bf16[72,512]{1,0:T(8,128)(2,1)S(1)} %get-tuple-element.9), channel_id=1, source_target_pairs={{7,0},{4,1},{5,2},{6,3},{11,4},{8,5},{9,6},{10,7},{15,8},{12,9},{1... | collective-permute-start | bytes 221192 | tf_op jit(solution)/shard_map/ppermute | solution.py:221
  43.1 3.0 %collective-permute-start.5 = (bf16[72,512]{1,0:T(8,128)(2,1)S(1)}, bf16[72,512]{1,0:T(8,128)(2,1)S(1)}, u32[]{:S(2)}, u32[]{:S(2)}) collective-permute-start(bf16[72,512]{1,0:T(8,128)(2,1)S(1)} %get-tuple-element.10), channel_id=1, source_target_pairs={{1,4},{2,5},{3,6},{0,7},{5,8},{6,9},{7,10},{4,11},{9,12},{10,13},{... | collective-permute-start | bytes 221192 | tf_op jit(solution)/shard_map/ppermute | solution.py:221
  46.1 0.1 pad_add_fusion
  46.1 0.1 and_not_fusion
  46.2 0.9 slice.21
  47.1 14.7 %collective-permute-done.7.br_ref = bf16[72,512]{1,0:T(8,128)(2,1)S(1)} collective-permute-done((bf16[72,512]{1,0:T(8,128)(2,1)S(1)}, bf16[72,512]{1,0:T(8,128)(2,1)S(1)}, u32[]{:S(2)}, u32[]{:S(2)}) %collective-permute-start.7) | collective-permute-done | bytes 73760 | tf_op jit(solution)/shard_map/ppermute | solution.py:221
  61.8 6.4 %collective-permute-start.4 = (bf16[72,512]{1,0:T(8,128)(2,1)S(1)}, bf16[72,512]{1,0:T(8,128)(2,1)S(1)}, u32[]{:S(2)}, u32[]{:S(2)}) collective-permute-start(bf16[72,512]{1,0:T(8,128)(2,1)S(1)} %get-tuple-element.10), channel_id=1, source_target_pairs={{3,4},{0,5},{1,6},{2,7},{7,8},{4,9},{5,10},{6,11},{11,12},{8,13},{... | collective-permute-start | bytes 221192 | tf_op jit(solution)/shard_map/ppermute | solution.py:221
  68.2 0.0 collective-permute-done.6.bl_ref
  68.2 0.0 copy-start.5
  68.2 0.1 collective-permute-start.3
  68.3 0.0 collective-permute-done.5.tr_ref
  68.3 0.0 copy-start.6
  68.3 1.7 %collective-permute-start.2 = (bf16[2,72,512]{2,1,0:T(8,128)(2,1)S(1)}, bf16[2,72,512]{2,1,0:T(8,128)(2,1)S(1)}, u32[]{:S(2)}, u32[]{:S(2)}) collective-permute-start(bf16[2,72,512]{2,1,0:T(8,128)(2,1)S(1)} %slice.21), channel_id=1, source_target_pairs={{3,0},{0,1},{1,2},{2,3},{7,4},{4,5},{5,6},{6,7},{11,8},{8,9},{9,10... | collective-permute-start | bytes 442376 | tf_op jit(solution)/shard_map/ppermute | solution.py:221
  70.0 0.7 and_select_fusion.bias_ref
  70.7 0.0 collective-permute-done.4.tl_ref
  70.7 4.0 %collective-permute-done.3.right_ref = bf16[2,72,512]{2,1,0:T(8,128)(2,1)S(1)} collective-permute-done((bf16[2,72,512]{2,1,0:T(8,128)(2,1)S(1)}, bf16[2,72,512]{2,1,0:T(8,128)(2,1)S(1)}, u32[]{:S(2)}, u32[]{:S(2)}) %collective-permute-start.3) | collective-permute-done | bytes 147488 | tf_op jit(solution)/shard_map/ppermute | solution.py:221
  74.7 0.0 collective-permute-done.2.left_ref
  74.7 0.0 collective-permute-done.1.bot_ref
  74.7 0.0 collective-permute-done.top_ref
  74.7 0.0 copy-start.1
  74.7 0.0 copy-done.4
  74.8 0.6 copy-done.2
  75.3 0.1 copy-done.3
  75.4 0.2 copy-done
  75.6 0.2 copy-done.1
  75.8 36.0 %shifted.1 = bf16[2,576,512]{2,1,0:T(8,128)(2,1)} custom-call(bf16[2,576,512]{2,1,0:T(8,128)(2,1)} %get-tuple-element.7.x_ref, bf16[2,576,512]{2,1,0:T(8,128)(2,1)} %get-tuple-element.8.n_ref, bf16[576,512]{1,0:T(8,128)(2,1)} %copy-done.1, bf16[576,512]{1,0:T(8,128)(2,1)} %copy-done, bf16[2,72,512]{2,1,0:T(8,128)(2,1)} %copy-done.3, ...), custom_call_target="tpu_custom_call" | custom-call | tf_op jit(solution)/shard_map/shifted/pallas_call | solution.py:239
  (12 shorter events, 0.0 us)
Async XLA Ops:
  28.2 17.9 %copy-start.9 = (pred[144]{0:T(512)(128)(4,1)S(1)}, pred[144]{0:T(512)(128)(4,1)}, u32[]{:S(2)}) copy-start(pred[144]{0:T(512)(128)(4,1)} %constant.28) | copy-start | bytes 436
  28.2 41.8 %copy-start.8 = (pred[72,144]{1,0:T(8,128)(4,1)S(1)}, pred[72,144]{1,0:T(8,128)(4,1)}, u32[]{:S(2)}) copy-start(pred[72,144]{1,0:T(8,128)(4,1)} %constant.27) | copy-start | bytes 31108
  29.6 45.1 %collective-permute-start.1 = (bf16[576,512]{1,0:T(8,128)(2,1)S(1)}, bf16[576,512]{1,0:T(8,128)(2,1)S(1)}, u32[]{:S(2)}, u32[]{:S(2)}) collective-permute-start(bf16[576,512]{1,0:T(8,128)(2,1)S(1)} %get-tuple-element.11), channel_id=1, source_target_pairs={{4,0},{5,1},{6,2},{7,3},{8,4},{9,5},{10,6},{11,7},{12,8},{13,9},{1... | collective-permute-start | bytes 1769480 | tf_op jit(solution)/shard_map/ppermute | solution.py:221
  31.7 43.0 %collective-permute-start = (bf16[576,512]{1,0:T(8,128)(2,1)S(1)}, bf16[576,512]{1,0:T(8,128)(2,1)S(1)}, u32[]{:S(2)}, u32[]{:S(2)}) collective-permute-start(bf16[576,512]{1,0:T(8,128)(2,1)S(1)} %get-tuple-element.12), channel_id=1, source_target_pairs={{0,4},{1,5},{2,6},{3,7},{4,8},{5,9},{6,10},{7,11},{8,12},{9,13},{1... | collective-permute-start | bytes 1769480 | tf_op jit(solution)/shard_map/ppermute | solution.py:221
  36.7 25.1 %collective-permute-start.7 = (bf16[72,512]{1,0:T(8,128)(2,1)S(1)}, bf16[72,512]{1,0:T(8,128)(2,1)S(1)}, u32[]{:S(2)}, u32[]{:S(2)}) collective-permute-start(bf16[72,512]{1,0:T(8,128)(2,1)S(1)} %get-tuple-element.9), channel_id=1, source_target_pairs={{5,0},{6,1},{7,2},{4,3},{9,4},{10,5},{11,6},{8,7},{13,8},{14,9},{1... | collective-permute-start | bytes 221192 | tf_op jit(solution)/shard_map/ppermute | solution.py:221
  39.1 29.1 %collective-permute-start.6 = (bf16[72,512]{1,0:T(8,128)(2,1)S(1)}, bf16[72,512]{1,0:T(8,128)(2,1)S(1)}, u32[]{:S(2)}, u32[]{:S(2)}) collective-permute-start(bf16[72,512]{1,0:T(8,128)(2,1)S(1)} %get-tuple-element.9), channel_id=1, source_target_pairs={{7,0},{4,1},{5,2},{6,3},{11,4},{8,5},{9,6},{10,7},{15,8},{12,9},{1... | collective-permute-start | bytes 221192 | tf_op jit(solution)/shard_map/ppermute | solution.py:221
  43.1 25.2 %collective-permute-start.5 = (bf16[72,512]{1,0:T(8,128)(2,1)S(1)}, bf16[72,512]{1,0:T(8,128)(2,1)S(1)}, u32[]{:S(2)}, u32[]{:S(2)}) collective-permute-start(bf16[72,512]{1,0:T(8,128)(2,1)S(1)} %get-tuple-element.10), channel_id=1, source_target_pairs={{1,4},{2,5},{3,6},{0,7},{5,8},{6,9},{7,10},{4,11},{9,12},{10,13},{... | collective-permute-start | bytes 221192 | tf_op jit(solution)/shard_map/ppermute | solution.py:221
  61.8 12.9 %copy-start.4 = (bf16[72,512]{1,0:T(8,128)(2,1)}, bf16[72,512]{1,0:T(8,128)(2,1)S(1)}, u32[]{:S(2)}) copy-start(bf16[72,512]{1,0:T(8,128)(2,1)S(1)} %collective-permute-done.7.br_ref) | copy-start | bytes 221188
  61.8 8.9 %collective-permute-start.4 = (bf16[72,512]{1,0:T(8,128)(2,1)S(1)}, bf16[72,512]{1,0:T(8,128)(2,1)S(1)}, u32[]{:S(2)}, u32[]{:S(2)}) collective-permute-start(bf16[72,512]{1,0:T(8,128)(2,1)S(1)} %get-tuple-element.10), channel_id=1, source_target_pairs={{3,4},{0,5},{1,6},{2,7},{7,8},{4,9},{5,10},{6,11},{11,12},{8,13},{... | collective-permute-start | bytes 221192 | tf_op jit(solution)/shard_map/ppermute | solution.py:221
  68.2 6.5 %copy-start.5 = (bf16[72,512]{1,0:T(8,128)(2,1)}, bf16[72,512]{1,0:T(8,128)(2,1)S(1)}, u32[]{:S(2)}) copy-start(bf16[72,512]{1,0:T(8,128)(2,1)S(1)} %collective-permute-done.6.bl_ref) | copy-start | bytes 221188
  68.2 6.5 %collective-permute-start.3 = (bf16[2,72,512]{2,1,0:T(8,128)(2,1)S(1)}, bf16[2,72,512]{2,1,0:T(8,128)(2,1)S(1)}, u32[]{:S(2)}, u32[]{:S(2)}) collective-permute-start(bf16[2,72,512]{2,1,0:T(8,128)(2,1)S(1)} %slice.21), channel_id=1, source_target_pairs={{1,0},{2,1},{3,2},{0,3},{5,4},{6,5},{7,6},{4,7},{9,8},{10,9},{11,1... | collective-permute-start | bytes 442376 | tf_op jit(solution)/shard_map/ppermute | solution.py:221
  68.3 6.5 %copy-start.6 = (bf16[72,512]{1,0:T(8,128)(2,1)}, bf16[72,512]{1,0:T(8,128)(2,1)S(1)}, u32[]{:S(2)}) copy-start(bf16[72,512]{1,0:T(8,128)(2,1)S(1)} %collective-permute-done.5.tr_ref) | copy-start | bytes 221188
  68.3 6.4 %collective-permute-start.2 = (bf16[2,72,512]{2,1,0:T(8,128)(2,1)S(1)}, bf16[2,72,512]{2,1,0:T(8,128)(2,1)S(1)}, u32[]{:S(2)}, u32[]{:S(2)}) collective-permute-start(bf16[2,72,512]{2,1,0:T(8,128)(2,1)S(1)} %slice.21), channel_id=1, source_target_pairs={{3,0},{0,1},{1,2},{2,3},{7,4},{4,5},{5,6},{6,7},{11,8},{8,9},{9,10... | collective-permute-start | bytes 442376 | tf_op jit(solution)/shard_map/ppermute | solution.py:221
  70.7 4.1 %copy-start.7 = (bf16[72,512]{1,0:T(8,128)(2,1)}, bf16[72,512]{1,0:T(8,128)(2,1)S(1)}, u32[]{:S(2)}) copy-start(bf16[72,512]{1,0:T(8,128)(2,1)S(1)} %collective-permute-done.4.tl_ref) | copy-start | bytes 221188
  74.7 0.7 copy-start.2
  74.7 0.7 copy-start.3
  74.7 0.9 copy-start
  74.7 1.1 copy-start.1
where the time goes:
time: 112 us
  Pallas kernels  64.2 us (57%)
  starting transfers between devices  23.6 us (21%)
  waiting for transfers between devices  18.7 us (17%)
  local copies, waits for them, and re-layouts  4.26 us (4%)
    pallas_call x1, Pallas kernels, shards(): pl.pallas_call(block1, grid=(1,), in_specs=[whole(a.shape) for a in (x1,...  36 us
    pallas_call x1, Pallas kernels, shards(): pl.pallas_call(block0, grid=(1,), in_specs=[whole((2, half, channels)), w...  28.2 us
    ppermute x8, starting transfers between devices, move(): return lax.ppermute(block, ('lat', 'lon'), route)  23.6 us
    ppermute x8, waiting for transfers between devices, move(): return lax.ppermute(block, ('lat', 'lon'), route)  18.7 us
  transfers between devices with their start and end apart: 8, of which 2 were waited for; matrix products, arithmetic and copies ran while one was open for 2% of the time, Pallas kernels for 0%

commit v1 on v0

v1 whole, which is shorter than its diff:
```python
import functools

import jax
import jax.numpy as jnp
import numpy as np
from jax import lax
from jax.experimental import pallas as pl
from jax.experimental.pallas import tpu as pltpu
from jax.sharding import PartitionSpec as P

HEADS = 16
WY = 12
WX = 6
SY = 6
SX = 3
EPSILON = 1e-05
NEGATIVE = -1e30
BF = jnp.bfloat16
F32 = jnp.float32
UNIT = 36
WIDTH0 = 128
WIDTH1 = 256
EXP_SCALE = float(32.0 ** -0.5 * np.log2(np.e))


def norm(values, gain_row):
    centered = values - jnp.mean(values, axis=-1, keepdims=True)
    variance = jnp.mean(centered * centered, axis=-1, keepdims=True)
    return (centered * lax.rsqrt(variance + EPSILON) * gain_row).astype(BF)


def dot(a, b):
    return jnp.dot(a, b, preferred_element_type=F32)


def attend(q, k, v, bias, width):
    n, channels = q.shape
    head = channels // HEADS
    count = width // head
    lane = lax.broadcasted_iota(jnp.int32, (1, width), 1) // head
    lanes = lax.broadcasted_iota(jnp.int32, (n, width), 1) // head
    pieces = []
    for g in range(channels // width):
        cut = slice(width * g, width * (g + 1))
        qg = q[:, cut]
        stacked = jnp.concatenate(
            [qg * (lane == j).astype(F32) for j in range(count)], axis=0
        ).astype(BF)
        s = lax.dot_general(
            stacked, k[:, cut], (((1,), (1,)), ((), ())), preferred_element_type=F32
        )
        if bias is not None:
            s = s + jnp.concatenate([bias] * count, axis=0)
        p = jnp.exp2((s - jnp.max(s, axis=-1, keepdims=True)) * EXP_SCALE).astype(BF)
        vg = v[:, cut]
        o = dot(p, jnp.concatenate([vg, jnp.ones((vg.shape[0], 128), BF)], axis=1))
        scale = 1.0 / o[:, width:]
        if width > 128:
            scale = jnp.concatenate([scale] * (width // 128), axis=1)
        o = o[:, :width] * scale
        total = o[:n]
        for j in range(1, count):
            total = jnp.where(lanes == j, o[j * n : (j + 1) * n], total)
        pieces.append(total)
    return jnp.concatenate(pieces, axis=1)


def finish(x, attended, gain_row, w_proj, w_in, w_out):
    mixed = (x.astype(F32) + dot(attended, w_proj)).astype(BF)
    normed = norm(mixed.astype(F32), gain_row)
    h = dot(normed, w_in)
    h = jax.nn.gelu(h, approximate=True).astype(BF)
    return mixed.astype(F32) + dot(h, w_out)


def block0(keep, side_ref, x_ref, *refs):
    *halos, perm_ref, gains_ref, wqkv_ref, wproj_ref, win_ref, wout_ref = refs[:-7]
    x1_ref, cross_ref, same_ref, xs, qkv, att, xf = refs[-7:]
    tokens, channels = xs.shape
    half = tokens // 2
    strips = half // 72
    quarter = x_ref.shape[1] // 2
    perm = perm_ref[...]
    parts = []
    for r in range(2):
        nat = [x_ref[z, quarter * r : quarter * (r + 1)] for z in range(2)]
        if halos:
            nat.append(
                jnp.concatenate([h[r].astype(F32) for h in halos], axis=0).astype(BF)
            )
        nat = jnp.concatenate(nat, axis=0)
        parts.append(dot(perm, nat).reshape(strips, 72, channels))
    x = jnp.concatenate(parts, axis=1).reshape(tokens, channels)
    xs[...] = x.astype(BF)
    qkv[...] = dot(norm(x, gains_ref[0:1]), wqkv_ref[0]).astype(BF)

    def window(i, _):
        at = pl.ds(pl.multiple_of(i * 144, 16), 144)
        q = qkv[at, :channels].astype(F32)
        k, v = qkv[at, channels : 2 * channels], qkv[at, 2 * channels :]
        att[at] = attend(q, k, v, None, WIDTH0).astype(BF)
        return 0

    lax.fori_loop(0, strips, window, 0)
    new = finish(xs[...], att[...], gains_ref[1:2], wproj_ref[0], win_ref[0], wout_ref[0])
    new = new.reshape(strips, 2, 72, channels)
    for r in range(2):
        xf[r] = new[:, r].reshape(half, channels)
    odd = side_ref[0]
    for g, n_ref in ((0, cross_ref), (1, same_ref)):
        mine = pltpu.roll(xf[jnp.where(odd == 0, g, 1 - g)], UNIT, 0).astype(BF)
        x1_ref[g] = mine[:keep]
        n_ref[...] = norm(mine.astype(F32), gains_ref[2:3])[:keep]


def blocks(rows):
    return rows.astype(F32).reshape(-1, 72, rows.shape[-1])


def windows(own, far, bias_ref, wqkv_ref, lhs, qs, kv, os):
    count, _, channels = own.shape
    lhs[...] = jnp.concatenate([own, far], axis=1).reshape(count * 144, channels).astype(BF)
    q = dot(own.reshape(count * 72, channels).astype(BF), wqkv_ref[0, :, :channels])
    qs[...] = q.astype(BF).astype(F32).reshape(count, 72, channels)
    rows = count * 72

    def project(i, _):
        at = pl.ds(pl.multiple_of(i * rows, 16), rows)
        kv[at] = dot(lhs[at], wqkv_ref[0, :, channels:]).astype(BF)
        return 0

    lax.fori_loop(0, 2, project, 0)

    def window(i, _):
        at = pl.ds(pl.multiple_of(i * 144, 16), 144)
        bias = bias_ref[i // (count // 2)]
        os[i] = attend(qs[i], kv[at, :channels], kv[at, channels:], bias, WIDTH1)
        return 0

    lax.fori_loop(0, count, window, 0)


def early(x_ref, cross_ref, same_ref, far_cross_ref, far_same_ref, bias_ref,
          gains_ref, wqkv_ref, wproj_ref, win_ref, wout_ref, out_ref, lhs, qs, kv, os):
    channels = x_ref.shape[-1]

    def pair(a_ref, b_ref):
        return jnp.concatenate([blocks(a_ref[...])[1:], blocks(b_ref[...])[1:]], axis=0)

    own, far = pair(cross_ref, same_ref), pair(far_cross_ref, far_same_ref)
    windows(own, far, bias_ref, wqkv_ref, lhs, qs, kv, os)
    rows = own.shape[0] * 72
    x = jnp.concatenate([blocks(x_ref[g])[1:] for g in range(2)], axis=0).reshape(rows, channels)
    attended = os[...].reshape(rows, channels).astype(BF)
    out_ref[...] = finish(
        x, attended, gains_ref[3:4], wproj_ref[0], win_ref[0], wout_ref[0]
    ).astype(BF)


def late(side_ref, done_ref, xa_ref, xb_ref, ca_ref, sa_ref, cb_ref, sb_ref,
         fca_ref, fsa_ref, fcb_ref, fsb_ref, bias_ref,
         perm_ref, gains_ref, wqkv_ref, wproj_ref, win_ref, wout_ref,
         out_ref, lhs, qs, kv, os, tile_ref):
    channels = xa_ref.shape[-1]
    first = lax.broadcasted_iota(jnp.int32, (72, channels), 0) < UNIT

    def extend(a, b):
        a, b = blocks(a), blocks(b)
        mid, lead = jnp.where(first, a[0], b[0]), jnp.where(first, b[0], a[0])
        return jnp.concatenate([mid[None], b[1:], lead[None]], axis=0)

    own = jnp.concatenate(
        [extend(ca_ref[...], cb_ref[...]), extend(sa_ref[...], sb_ref[...])], axis=0
    )
    far = jnp.concatenate(
        [extend(fca_ref[...], fcb_ref[...]), extend(fsa_ref[...], fsb_ref[...])], axis=0
    )
    windows(own, far, bias_ref, wqkv_ref, lhs, qs, kv, os)
    count = own.shape[0] // 2
    last = count - 2
    xs, atts = [], []
    for g in range(2):
        a, b = blocks(xa_ref[g]), blocks(xb_ref[g])
        o = os[count * g : count * (g + 1)]
        xs += [
            jnp.where(first, b[last], a[0])[None],
            jnp.where(first, a[0], b[0])[None],
            b[1:last],
        ]
        atts += [jnp.where(first, o[last], o[count - 1])[None], o[:last]]
    rows = (count - 1) * 72
    x = jnp.concatenate(xs, axis=0).reshape(2 * rows, channels)
    attended = jnp.concatenate(atts, axis=0).reshape(2 * rows, channels).astype(BF)
    new = finish(x, attended, gains_ref[3:4], wproj_ref[0], win_ref[0], wout_ref[0])
    ready = done_ref[...].astype(F32)
    share = ready.shape[0] // 2
    odd = side_ref[0]
    for g in range(2):
        tile_ref[:72] = new[rows * g : rows * g + 72]
        tile_ref[72 : 72 + share] = ready[share * g : share * (g + 1)]
        tile_ref[72 + share :] = new[rows * g + 72 : rows * (g + 1)]
        nat = dot(perm_ref[...], tile_ref[...].astype(BF)).astype(BF)
        quarter = nat.shape[0] // 2
        r = jnp.where(odd == 0, g, 1 - g)
        for z in range(2):
            out_ref[z, r] = nat[quarter * z : quarter * (z + 1)]


def orders(strips):
    unit, lev, row, col = np.meshgrid(
        np.arange(2 * strips), np.arange(2), np.arange(SY), np.arange(SX), indexing="ij"
    )
    breadth = WX * strips
    return (lev * SY * breadth + row * breadth + unit * SX + col).reshape(-1)


def whole(shape):
    return pl.BlockSpec(shape, lambda i, n=len(shape): (0,) * n)


def layer(shape, index):
    return pl.BlockSpec((1,) + shape[1:], lambda i: (index, 0, 0))


def tables(breadth):
    strips = breadth // WX
    order = orders(strips)
    half = order.size
    onehot = np.zeros((half, half), np.float32)
    onehot[np.arange(half), order] = 1.0
    cut = 72 * (strips // 2 + 1)
    halo = np.zeros((72, 72), np.float32)
    halo[np.arange(72), orders(1)] = 1.0
    rest = np.zeros((half - cut + 144, half + 144), np.float32)
    rest[: half - cut, :half] = onehot[cut:]
    rest[half - cut : half - cut + 72, half : half + 72] = halo
    rest[half - cut + 72 :, half + 72 :] = halo
    made = (onehot[:cut], rest, np.roll(onehot, UNIT, axis=0).T)
    return tuple(jnp.asarray(m, BF) for m in made)


PARAMS = pltpu.CompilerParams(
    dimension_semantics=("arbitrary",), vmem_limit_bytes=56 * 1024 * 1024
)


def call(body, name, scalars, arrays, extra, weights, index, outs, scratch):
    return pl.pallas_call(
        body,
        grid=(1,),
        in_specs=[pl.BlockSpec(memory_space=pltpu.SMEM) for _ in scalars]
        + [whole(a.shape) for a in arrays + extra]
        + [layer(w.shape, index) for w in weights],
        out_specs=[whole(o) for o in outs],
        out_shape=[jax.ShapeDtypeStruct(o, BF) for o in outs],
        scratch_shapes=scratch,
        compiler_params=PARAMS,
        name=name,
    )(*scalars, *arrays, *extra, *weights)


def regular(side, tokens, halos, perm, gains, weights):
    channels = tokens.shape[-1]
    half = perm.shape[0]
    keep = half - 72 if halos else half
    outs = [(2, keep, channels), (keep, channels), (keep, channels)]
    scratch = [
        pltpu.VMEM((2 * half, channels), BF),
        pltpu.VMEM((2 * half, 3 * channels), BF),
        pltpu.VMEM((2 * half, channels), BF),
        pltpu.VMEM((2, half, channels), F32),
    ]
    body = functools.partial(block0, keep)
    name = "regular_b" if halos else "regular_a"
    return call(body, name, [side], [tokens, *halos], [perm, gains], weights, 0, outs, scratch)


def room(count, channels):
    return [
        pltpu.VMEM((count * 144, channels), BF),
        pltpu.VMEM((count, 72, channels), F32),
        pltpu.VMEM((count * 144, 2 * channels), BF),
        pltpu.VMEM((count, 72, channels), F32),
    ]


def shifted_early(arrays, gains, weights):
    _, half, channels = arrays[0].shape
    count = 2 * (half // 72 - 1)
    outs = [(count * 72, channels)]
    return call(early, "early", [], arrays, [gains], weights, 1, outs, room(count, channels))[0]


def shifted_late(side, arrays, perm, gains, weights):
    _, kept, channels = arrays[2].shape
    count = 2 * (kept // 72 + 1)
    half = perm.shape[0]
    outs = [(2, 2, half // 2, channels)]
    scratch = room(count, channels) + [pltpu.VMEM((half, channels), F32)]
    return call(late, "late", [side], arrays, [perm, gains], weights, 1, outs, scratch)[0]


def shards(tokens, gains, w_qkv, w_proj, w_in, w_out):
    levels, height, breadth, channels = tokens.shape
    perm_a, perm_b, back = tables(breadth)
    weights = (w_qkv, w_proj, w_in, w_out)
    lats, lons = lax.axis_size("lat"), lax.axis_size("lon")
    place = lax.axis_index("lat")
    side = (place % 2).astype(jnp.int32).reshape(1)

    def column(part):
        part = part.reshape(levels, 2, SY, WX, channels).transpose(1, 0, 2, 3, 4)
        return part.reshape(2, 72, channels)

    def beside(part, distance):
        route = [((x + distance) % lons, x) for x in range(lons)]
        return lax.ppermute(column(part), "lon", route)

    def swap(block, first):
        route = []
        for y in range(first, lats - 1, 2):
            route += [(y, y + 1), (y + 1, y)]
        return lax.ppermute(block, "lat", route)

    left = beside(tokens[:, :, breadth - WX :], -1)
    right = beside(tokens[:, :, :WX], 1)
    tile = tokens.reshape(2, -1, channels)
    xa, ca, sa = regular(side, tile, [], perm_a, gains, weights)
    fca, fsa = swap(ca, 1), swap(sa, 0)
    xb, cb, sb = regular(side, tile, [right, left], perm_b, gains, weights)
    fcb, fsb = swap(cb, 1), swap(sb, 0)

    token = np.arange(72)
    lev = token % UNIT // (UNIT // 2)
    same = np.tile(lev[:, None] == lev[None, :], (1, 2))
    far = np.arange(144) >= 72
    step = 1 - 2 * (place % 2)
    partners = jnp.stack([place - step, place + step])
    dead = (partners < 0) | (partners >= lats)
    allowed = same[None] & ~(dead[:, None, None] & far[None, None, :])
    bias = jnp.where(allowed, 0.0, NEGATIVE).astype(F32)
    done = shifted_early([xa, ca, sa, fca, fsa, bias], gains, weights)
    out = shifted_late(
        side, [done, xa, xb, ca, sa, cb, sb, fca, fsa, fcb, fsb, bias], back, gains, weights
    )
    return out.reshape(tokens.shape)


def solution(mesh):
    in_specs = (P(None, "lat", "lon", None), P(), P(), P(), P(), P())
    out_specs = P(None, "lat", "lon", None)
    return jax.shard_map(shards, mesh=mesh, in_specs=in_specs, out_specs=out_specs, check_vma=False)
```

time: 112 us -> 81.5 us (0.73)
  the two profiles are of different devices: /device:TPU:13 before, /device:TPU:0 now
where the time goes in v1:
time: 81.5 us; the launch traced here: 81.3 us
  Pallas kernels  63.1 us (77%)
  starting transfers between devices  12.9 us (16%)
  local copies, waits for them, and re-layouts  4.38 us (5%)
  other arithmetic  0.82 us (1%)
    pallas_call x4, Pallas kernels, call(): pl.pallas_call(body, grid=(1,), in_specs=[pl.BlockSpec(memory_space=pltpu...  63.1 us
    ppermute x4, starting transfers between devices, swap(): return lax.ppermute(block, 'lat', route)  10.4 us
    unnamed x16, local copies, waits for them, and re-layouts  2.97 us
    ppermute x2, starting transfers between devices, beside(): return lax.ppermute(column(part), 'lon', route)  2.49 us
  transfers between devices with their start and end apart: 6, of which 0 were waited for; matrix products, arithmetic and copies ran while one was open for 1% of the time, Pallas kernels for 55%

profile of v1, /device:TPU:0, one launch (start us, length us, event | category | flops | bytes accessed | tf_op | source)
XLA Modules:
  0.0 81.3 jit_solution(1719740757741722934)
XLA Ops:
  0.0 1.1 %fusion = (bf16[2,12,6,512]{3,2,1,0:T(8,128)(2,1)S(1)}, bf16[2,12,6,512]{3,2,1,0:T(8,128)(2,1)S(1)}) fusion(bf16[2,12,48,512]{3,2,1,0:T(8,128)(2,1)} %param.11), kind=kLoop, calls=%fused_computation.3 | loop fusion | bytes 589824 | tf_op jit(solution)/shard_map/slice | solution.py:325
  1.1 0.2 copy.14
  1.3 2.4 %collective-permute-start.2 = (bf16[2,72,512]{2,1,0:T(8,128)(2,1)S(1)}, bf16[2,72,512]{2,1,0:T(8,128)(2,1)S(1)}, u32[]{:S(2)}, u32[]{:S(2)}) collective-permute-start(bf16[2,72,512]{2,1,0:T(8,128)(2,1)S(1)} %copy.15), channel_id=1, source_target_pairs={{1,0},{2,1},{3,2},{0,3},{5,4},{6,5},{7,6},{4,7},{9,8},{10,9},{11,1... | collective-permute-start | bytes 442376 | tf_op jit(solution)/shard_map/ppermute | solution.py:317
  3.7 0.2 copy.16
  3.9 0.1 collective-permute-start.3
  4.0 14.9 %regular_a.1 = (bf16[2,360,512]{2,1,0:T(8,128)(2,1)}, bf16[360,512]{1,0:T(8,128)(2,1)}, bf16[360,512]{1,0:T(8,128)(2,1)}) custom-call(s32[1]{0:T(128)} %bitcast.side_ref, bf16[2,576,512]{2,1,0:T(8,128)(2,1)} %bitcast.13, bf16[360,576]{1,0:T(8,128)(2,1)} %constant.39.clone.refs_0_, f32[4,512]{1,0:T(4,128)} %gains_ref.3, bf16[2,512,1536]{2,1,0:T(8,128)(2,1)} %wqkv_ref.3, ...), custom_call_target="tpu_custom_call" | custom-call | tf_op jit(solution)/shard_map/regular_a/pallas_call | solution.py:248
  18.8 0.9 %collective-permute-start = (bf16[360,512]{1,0:T(8,128)(2,1)}, bf16[360,512]{1,0:T(8,128)(2,1)S(1)}, u32[]{:S(2)}, u32[]{:S(2)}) collective-permute-start(bf16[360,512]{1,0:T(8,128)(2,1)} %get-tuple-element.12.cross_ref.ca_ref), channel_id=1, source_target_pairs={{4,8},{8,4},{12,16},{16,12},{20,24},{24,20},{5,9},{9,5},{13,17},{1... | collective-permute-start | bytes 1105928 | tf_op jit(solution)/shard_map/ppermute | solution.py:323
  19.7 4.3 %collective-permute-start.1 = (bf16[360,512]{1,0:T(8,128)(2,1)}, bf16[360,512]{1,0:T(8,128)(2,1)S(1)}, u32[]{:S(2)}, u32[]{:S(2)}) collective-permute-start(bf16[360,512]{1,0:T(8,128)(2,1)} %get-tuple-element.13.same_ref.sa_ref), channel_id=1, source_target_pairs={{0,4},{4,0},{8,12},{12,8},{16,20},{20,16},{24,28},{28,24},{1,5},{5... | collective-permute-start | bytes 1105928 | tf_op jit(solution)/shard_map/ppermute | solution.py:323
  24.0 0.1 compare_or_fusion
  24.1 0.0 collective-permute-done.2.refs_0_
  24.1 0.0 copy-start.4
  24.1 0.0 collective-permute-done.3.refs_1_
  24.1 0.6 copy-done.4
  24.8 0.7 copy-done.5
  25.4 14.8 %regular_b.1 = (bf16[2,288,512]{2,1,0:T(8,128)(2,1)}, bf16[288,512]{1,0:T(8,128)(2,1)}, bf16[288,512]{1,0:T(8,128)(2,1)}) custom-call(s32[1]{0:T(128)} %bitcast.side_ref, bf16[2,576,512]{2,1,0:T(8,128)(2,1)} %bitcast.14, bf16[2,72,512]{2,1,0:T(8,128)(2,1)} %copy-done.4, bf16[2,72,512]{2,1,0:T(8,128)(2,1)} %copy-done.5, ...), custom_call_target="tpu_custom_call" | custom-call | tf_op jit(solution)/shard_map/regular_b/pallas_call | solution.py:248
  40.2 0.9 %collective-permute-start.4 = (bf16[288,512]{1,0:T(8,128)(2,1)}, bf16[288,512]{1,0:T(8,128)(2,1)S(1)}, u32[]{:S(2)}, u32[]{:S(2)}) collective-permute-start(bf16[288,512]{1,0:T(8,128)(2,1)} %get-tuple-element.15.cb_ref), channel_id=1, source_target_pairs={{4,8},{8,4},{12,16},{16,12},{20,24},{24,20},{5,9},{9,5},{13,17},{1... | collective-permute-start | bytes 884744 | tf_op jit(solution)/shard_map/ppermute | solution.py:323
  41.1 4.3 %collective-permute-start.5 = (bf16[288,512]{1,0:T(8,128)(2,1)}, bf16[288,512]{1,0:T(8,128)(2,1)S(1)}, u32[]{:S(2)}, u32[]{:S(2)}) collective-permute-start(bf16[288,512]{1,0:T(8,128)(2,1)} %get-tuple-element.16.sb_ref), channel_id=1, source_target_pairs={{0,4},{4,0},{8,12},{12,8},{16,20},{20,16},{24,28},{28,24},{1,5},{5... | collective-permute-start | bytes 884744 | tf_op jit(solution)/shard_map/ppermute | solution.py:323
  45.5 0.0 copy-done.7
  45.5 0.1 and_not_fusion
  45.5 0.0 copy-done.6
  45.6 0.7 and_select_fusion.bias_ref
  46.2 0.0 collective-permute-done.far_cross_ref.fca_ref
  46.2 0.0 collective-permute-done.1.far_same_ref.fsa_ref
  46.2 0.0 copy-start.1
  46.2 0.7 copy-done
  47.0 0.1 copy-done.1
  47.1 14.7 %early.1.done_ref = bf16[576,512]{1,0:T(8,128)(2,1)} custom-call(bf16[2,360,512]{2,1,0:T(8,128)(2,1)} %get-tuple-element.11.x_ref.xa_ref, bf16[360,512]{1,0:T(8,128)(2,1)} %get-tuple-element.12.cross_ref.ca_ref, bf16[360,512]{1,0:T(8,128)(2,1)} %get-tuple-element.13.same_ref.sa_ref, bf16[360,512]{1,0:T(8,128)(2,1)} %copy-done, bf16[360,512]{1,0:T(8,128)(2,1)} %copy-done.1, ...), custom_call_target="tpu_custom_call" | custom-call | tf_op jit(solution)/shard_map/early/pallas_call | solution.py:248
  61.8 0.0 collective-permute-done.4.fcb_ref
  61.8 0.0 collective-permute-done.5.fsb_ref
  61.8 0.7 copy-done.2
  62.5 0.1 copy-done.3
  62.6 18.7 %late.1 = bf16[2,2,288,512]{3,2,1,0:T(8,128)(2,1)} custom-call(s32[1]{0:T(128)} %bitcast.side_ref, bf16[576,512]{1,0:T(8,128)(2,1)} %early.1.done_ref, bf16[2,360,512]{2,1,0:T(8,128)(2,1)} %get-tuple-element.11.x_ref.xa_ref, bf16[2,288,512]{2,1,0:T(8,128)(2,1)} %get-tuple-element.14.xb_ref, bf16[360,512]{1,0:T(8,128)(2,1)} %get-tuple-element.12.cross_ref.ca_ref, ...), custom_call_target="tpu_custom_call" | custom-call | tf_op jit(solution)/shard_map/late/pallas_call | solution.py:248
  (8 shorter events, 0.0 us)
Async XLA Ops:
  1.3 22.8 %collective-permute-start.2 = (bf16[2,72,512]{2,1,0:T(8,128)(2,1)S(1)}, bf16[2,72,512]{2,1,0:T(8,128)(2,1)S(1)}, u32[]{:S(2)}, u32[]{:S(2)}) collective-permute-start(bf16[2,72,512]{2,1,0:T(8,128)(2,1)S(1)} %copy.15), channel_id=1, source_target_pairs={{1,0},{2,1},{3,2},{0,3},{5,4},{6,5},{7,6},{4,7},{9,8},{10,9},{11,1... | collective-permute-start | bytes 442376 | tf_op jit(solution)/shard_map/ppermute | solution.py:317
  3.9 20.2 %collective-permute-start.3 = (bf16[2,72,512]{2,1,0:T(8,128)(2,1)S(1)}, bf16[2,72,512]{2,1,0:T(8,128)(2,1)S(1)}, u32[]{:S(2)}, u32[]{:S(2)}) collective-permute-start(bf16[2,72,512]{2,1,0:T(8,128)(2,1)S(1)} %copy.17), channel_id=1, source_target_pairs={{3,0},{0,1},{1,2},{2,3},{7,4},{4,5},{5,6},{6,7},{11,8},{8,9},{9,10... | collective-permute-start | bytes 442376 | tf_op jit(solution)/shard_map/ppermute | solution.py:317
  18.8 27.4 %collective-permute-start = (bf16[360,512]{1,0:T(8,128)(2,1)}, bf16[360,512]{1,0:T(8,128)(2,1)S(1)}, u32[]{:S(2)}, u32[]{:S(2)}) collective-permute-start(bf16[360,512]{1,0:T(8,128)(2,1)} %get-tuple-element.12.cross_ref.ca_ref), channel_id=1, source_target_pairs={{4,8},{8,4},{12,16},{16,12},{20,24},{24,20},{5,9},{9,5},{13,17},{1... | collective-permute-start | bytes 1105928 | tf_op jit(solution)/shard_map/ppermute | solution.py:323
  19.7 26.5 %collective-permute-start.1 = (bf16[360,512]{1,0:T(8,128)(2,1)}, bf16[360,512]{1,0:T(8,128)(2,1)S(1)}, u32[]{:S(2)}, u32[]{:S(2)}) collective-permute-start(bf16[360,512]{1,0:T(8,128)(2,1)} %get-tuple-element.13.same_ref.sa_ref), channel_id=1, source_target_pairs={{0,4},{4,0},{8,12},{12,8},{16,20},{20,16},{24,28},{28,24},{1,5},{5... | collective-permute-start | bytes 1105928 | tf_op jit(solution)/shard_map/ppermute | solution.py:323
  24.1 21.4 %copy-start.7 = (pred[144]{0:T(512)(128)(4,1)S(1)}, pred[144]{0:T(512)(128)(4,1)}, u32[]{:S(2)}) copy-start(pred[144]{0:T(512)(128)(4,1)} %constant.46) | copy-start | bytes 436
  24.1 21.5 %copy-start.6 = (pred[72,144]{1,0:T(8,128)(4,1)S(1)}, pred[72,144]{1,0:T(8,128)(4,1)}, u32[]{:S(2)}) copy-start(pred[72,144]{1,0:T(8,128)(4,1)} %constant.45) | copy-start | bytes 31108
  24.1 0.7 copy-start.4
  24.8 0.7 copy-start.5
  40.2 21.5 %collective-permute-start.4 = (bf16[288,512]{1,0:T(8,128)(2,1)}, bf16[288,512]{1,0:T(8,128)(2,1)S(1)}, u32[]{:S(2)}, u32[]{:S(2)}) collective-permute-start(bf16[288,512]{1,0:T(8,128)(2,1)} %get-tuple-element.15.cb_ref), channel_id=1, source_target_pairs={{4,8},{8,4},{12,16},{16,12},{20,24},{24,20},{5,9},{9,5},{13,17},{1... | collective-permute-start | bytes 884744 | tf_op jit(solution)/shard_map/ppermute | solution.py:323
  41.1 20.6 %collective-permute-start.5 = (bf16[288,512]{1,0:T(8,128)(2,1)}, bf16[288,512]{1,0:T(8,128)(2,1)S(1)}, u32[]{:S(2)}, u32[]{:S(2)}) collective-permute-start(bf16[288,512]{1,0:T(8,128)(2,1)} %get-tuple-element.16.sb_ref), channel_id=1, source_target_pairs={{0,4},{4,0},{8,12},{12,8},{16,20},{20,16},{24,28},{28,24},{1,5},{5... | collective-permute-start | bytes 884744 | tf_op jit(solution)/shard_map/ppermute | solution.py:323
  46.2 0.7 copy-start
  46.2 0.9 %copy-start.1 = (bf16[360,512]{1,0:T(8,128)(2,1)}, bf16[360,512]{1,0:T(8,128)(2,1)S(1)}, u32[]{:S(2)}) copy-start(bf16[360,512]{1,0:T(8,128)(2,1)S(1)} %collective-permute-done.1.far_same_ref.fsa_ref) | copy-start | bytes 1105924
  61.8 0.7 copy-start.2
  61.8 0.8 %copy-start.3 = (bf16[288,512]{1,0:T(8,128)(2,1)}, bf16[288,512]{1,0:T(8,128)(2,1)S(1)}, u32[]{:S(2)}) copy-start(bf16[288,512]{1,0:T(8,128)(2,1)S(1)} %collective-permute-done.5.fsb_ref) | copy-start | bytes 884740

commit v2 on v1

--- a/solution.py
+++ b/solution.py
@@ -14,6 +14,7 @@
 SY = 6
 SX = 3
 EPSILON = 1e-05
+LIMIT = 32 * 1024 * 1024
 NEGATIVE = -1e30
 BF = jnp.bfloat16
 F32 = jnp.float32
@@ -73,13 +74,37 @@
     return mixed.astype(F32) + dot(h, w_out)
 
 
-def block0(keep, side_ref, x_ref, *refs):
-    *halos, perm_ref, gains_ref, wqkv_ref, wproj_ref, win_ref, wout_ref = refs[:-7]
-    x1_ref, cross_ref, same_ref, xs, qkv, att, xf = refs[-7:]
+def fetch(moves, sems):
+    copies = [pltpu.make_async_copy(src, dst, sems.at[i]) for i, (src, dst) in enumerate(moves)]
+    for copy in copies:
+        copy.start()
+    return copies
+
+
+def weight_moves(refs, rooms, index):
+    wqkv, *others = refs
+    qkv_room, *other_rooms = rooms
+    cut = qkv_room.shape[0] // 2
+    parts = [slice(0, cut), slice(cut, 2 * cut)]
+    return [(wqkv.at[index, p], qkv_room.at[p]) for p in parts] + [
+        (w.at[index], room) for w, room in zip(others, other_rooms)
+    ]
+
+
+def block0(keep, side_ref, *refs):
+    *halos, gains_ref, x_far, perm_far, wqkv_far, wproj_far, win_far, wout_far = refs[:-14]
+    x1_ref, cross_ref, same_ref, xs, qkv, att, xf, x_ref, perm_ref = refs[-14:-5]
+    wqkv_ref, wproj_ref, win_ref, wout_ref, sems = refs[-5:]
+    moves = [(perm_far, perm_ref), (x_far.at[0], x_ref.at[0]), (x_far.at[1], x_ref.at[1])]
+    rooms = (wqkv_ref, wproj_ref, win_ref, wout_ref)
+    moves += weight_moves((wqkv_far, wproj_far, win_far, wout_far), rooms, 0)
+    copies = fetch(moves, sems)
     tokens, channels = xs.shape
     half = tokens // 2
     strips = half // 72
     quarter = x_ref.shape[1] // 2
+    for copy in copies[:3]:
+        copy.wait()
     perm = perm_ref[...]
     parts = []
     for r in range(2):
@@ -92,7 +117,10 @@
         parts.append(dot(perm, nat).reshape(strips, 72, channels))
     x = jnp.concatenate(parts, axis=1).reshape(tokens, channels)
     xs[...] = x.astype(BF)
-    qkv[...] = dot(norm(x, gains_ref[0:1]), wqkv_ref[0]).astype(BF)
+    normed = norm(x, gains_ref[0:1])
+    for copy in copies[3:5]:
+        copy.wait()
+    qkv[...] = dot(normed, wqkv_ref[...]).astype(BF)
 
     def window(i, _):
         at = pl.ds(pl.multiple_of(i * 144, 16), 144)
@@ -102,7 +130,9 @@
         return 0
 
     lax.fori_loop(0, strips, window, 0)
-    new = finish(xs[...], att[...], gains_ref[1:2], wproj_ref[0], win_ref[0], wout_ref[0])
+    for copy in copies[5:]:
+        copy.wait()
+    new = finish(xs[...], att[...], gains_ref[1:2], wproj_ref[...], win_ref[...], wout_ref[...])
     new = new.reshape(strips, 2, 72, channels)
     for r in range(2):
         xf[r] = new[:, r].reshape(half, channels)
@@ -117,16 +147,18 @@
     return rows.astype(F32).reshape(-1, 72, rows.shape[-1])
 
 
-def windows(own, far, bias_ref, wqkv_ref, lhs, qs, kv, os):
+def windows(own, far, bias_ref, wqkv_ref, copies, lhs, qs, kv, os):
     count, _, channels = own.shape
     lhs[...] = jnp.concatenate([own, far], axis=1).reshape(count * 144, channels).astype(BF)
-    q = dot(own.reshape(count * 72, channels).astype(BF), wqkv_ref[0, :, :channels])
+    for copy in copies:
+        copy.wait()
+    q = dot(own.reshape(count * 72, channels).astype(BF), wqkv_ref[:, :channels])
     qs[...] = q.astype(BF).astype(F32).reshape(count, 72, channels)
     rows = count * 72
 
     def project(i, _):
         at = pl.ds(pl.multiple_of(i * rows, 16), rows)
-        kv[at] = dot(lhs[at], wqkv_ref[0, :, channels:]).astype(BF)
+        kv[at] = dot(lhs[at], wqkv_ref[:, channels:]).astype(BF)
         return 0
 
     lax.fori_loop(0, 2, project, 0)
@@ -141,27 +173,36 @@
 
 
 def early(x_ref, cross_ref, same_ref, far_cross_ref, far_same_ref, bias_ref,
-          gains_ref, wqkv_ref, wproj_ref, win_ref, wout_ref, out_ref, lhs, qs, kv, os):
+          gains_ref, wqkv_far, wproj_far, win_far, wout_far, out_ref, lhs, qs, kv, os,
+          wqkv_ref, wproj_ref, win_ref, wout_ref, sems):
     channels = x_ref.shape[-1]
+    rooms = (wqkv_ref, wproj_ref, win_ref, wout_ref)
+    copies = fetch(weight_moves((wqkv_far, wproj_far, win_far, wout_far), rooms, 1), sems)
 
     def pair(a_ref, b_ref):
         return jnp.concatenate([blocks(a_ref[...])[1:], blocks(b_ref[...])[1:]], axis=0)
 
     own, far = pair(cross_ref, same_ref), pair(far_cross_ref, far_same_ref)
-    windows(own, far, bias_ref, wqkv_ref, lhs, qs, kv, os)
+    windows(own, far, bias_ref, wqkv_ref, copies[:2], lhs, qs, kv, os)
+    for copy in copies[2:]:
+        copy.wait()
     rows = own.shape[0] * 72
     x = jnp.concatenate([blocks(x_ref[g])[1:] for g in range(2)], axis=0).reshape(rows, channels)
     attended = os[...].reshape(rows, channels).astype(BF)
     out_ref[...] = finish(
-        x, attended, gains_ref[3:4], wproj_ref[0], win_ref[0], wout_ref[0]
+        x, attended, gains_ref[3:4], wproj_ref[...], win_ref[...], wout_ref[...]
     ).astype(BF)
 
 
 def late(side_ref, done_ref, xa_ref, xb_ref, ca_ref, sa_ref, cb_ref, sb_ref,
          fca_ref, fsa_ref, fcb_ref, fsb_ref, bias_ref,
-         perm_ref, gains_ref, wqkv_ref, wproj_ref, win_ref, wout_ref,
-         out_ref, lhs, qs, kv, os, tile_ref):
+         gains_ref, perm_far, wqkv_far, wproj_far, win_far, wout_far,
+         out_far, lhs, qs, kv, os, tile_ref, out_ref, perm_ref,
+         wqkv_ref, wproj_ref, win_ref, wout_ref, sems):
     channels = xa_ref.shape[-1]
+    rooms = (wqkv_ref, wproj_ref, win_ref, wout_ref)
+    moves = weight_moves((wqkv_far, wproj_far, win_far, wout_far), rooms, 1)
+    copies = fetch(moves + [(perm_far, perm_ref)], sems)
     first = lax.broadcasted_iota(jnp.int32, (72, channels), 0) < UNIT
 
     def extend(a, b):
@@ -175,7 +216,9 @@
     far = jnp.concatenate(
         [extend(fca_ref[...], fcb_ref[...]), extend(fsa_ref[...], fsb_ref[...])], axis=0
     )
-    windows(own, far, bias_ref, wqkv_ref, lhs, qs, kv, os)
+    windows(own, far, bias_ref, wqkv_ref, copies[:2], lhs, qs, kv, os)
+    for copy in copies[2:]:
+        copy.wait()
     count = own.shape[0] // 2
     last = count - 2
     xs, atts = [], []
@@ -191,10 +234,11 @@
     rows = (count - 1) * 72
     x = jnp.concatenate(xs, axis=0).reshape(2 * rows, channels)
     attended = jnp.concatenate(atts, axis=0).reshape(2 * rows, channels).astype(BF)
-    new = finish(x, attended, gains_ref[3:4], wproj_ref[0], win_ref[0], wout_ref[0])
+    new = finish(x, attended, gains_ref[3:4], wproj_ref[...], win_ref[...], wout_ref[...])
     ready = done_ref[...].astype(F32)
     share = ready.shape[0] // 2
     odd = side_ref[0]
+    sent = []
     for g in range(2):
         tile_ref[:72] = new[rows * g : rows * g + 72]
         tile_ref[72 : 72 + share] = ready[share * g : share * (g + 1)]
@@ -203,7 +247,12 @@
         quarter = nat.shape[0] // 2
         r = jnp.where(odd == 0, g, 1 - g)
         for z in range(2):
-            out_ref[z, r] = nat[quarter * z : quarter * (z + 1)]
+            out_ref[g, z] = nat[quarter * z : quarter * (z + 1)]
+            copy = pltpu.make_async_copy(out_ref.at[g, z], out_far.at[z, r], sems.at[2 * g + z])
+            copy.start()
+            sent.append(copy)
+    for copy in sent:
+        copy.wait()
 
 
 def orders(strips):
@@ -214,12 +263,8 @@
     return (lev * SY * breadth + row * breadth + unit * SX + col).reshape(-1)
 
 
-def whole(shape):
-    return pl.BlockSpec(shape, lambda i, n=len(shape): (0,) * n)
-
-
-def layer(shape, index):
-    return pl.BlockSpec((1,) + shape[1:], lambda i: (index, 0, 0))
+def near(array):
+    return pltpu.with_memory_space_constraint(array, pltpu.VMEM)
 
 
 def tables(breadth):
@@ -239,24 +284,23 @@
     return tuple(jnp.asarray(m, BF) for m in made)
 
 
-PARAMS = pltpu.CompilerParams(
-    dimension_semantics=("arbitrary",), vmem_limit_bytes=56 * 1024 * 1024
-)
-
-
-def call(body, name, scalars, arrays, extra, weights, index, outs, scratch):
+PARAMS = pltpu.CompilerParams(vmem_limit_bytes=LIMIT)
+
+
+def call(body, name, scalars, arrays, far, outs, scratch, keep=True):
+    vmem, hbm = (pl.BlockSpec(memory_space=m) for m in (pltpu.VMEM, pltpu.HBM))
+    weights = [pltpu.VMEM(w.shape[1:], BF) for w in far[-4:]]
     return pl.pallas_call(
         body,
-        grid=(1,),
         in_specs=[pl.BlockSpec(memory_space=pltpu.SMEM) for _ in scalars]
-        + [whole(a.shape) for a in arrays + extra]
-        + [layer(w.shape, index) for w in weights],
-        out_specs=[whole(o) for o in outs],
-        out_shape=[jax.ShapeDtypeStruct(o, BF) for o in outs],
-        scratch_shapes=scratch,
+        + [vmem for _ in arrays]
+        + [hbm for _ in far],
+        out_specs=[vmem if keep else hbm for _ in outs],
+        out_shape=[pltpu.VMEM(o, BF) if keep else pltpu.HBM(o, BF) for o in outs],
+        scratch_shapes=scratch + weights + [pltpu.SemaphoreType.DMA((8,))],
         compiler_params=PARAMS,
         name=name,
-    )(*scalars, *arrays, *extra, *weights)
+    )(*scalars, *[near(a) for a in arrays], *[pltpu.with_memory_space_constraint(a, pltpu.HBM) for a in far])
 
 
 def regular(side, tokens, halos, perm, gains, weights):
@@ -269,10 +313,14 @@
         pltpu.VMEM((2 * half, 3 * channels), BF),
         pltpu.VMEM((2 * half, channels), BF),
         pltpu.VMEM((2, half, channels), F32),
+        pltpu.VMEM(tokens.shape, BF),
+        pltpu.VMEM(perm.shape, BF),
     ]
     body = functools.partial(block0, keep)
     name = "regular_b" if halos else "regular_a"
-    return call(body, name, [side], [tokens, *halos], [perm, gains], weights, 0, outs, scratch)
+    return call(
+        body, name, [side], [*halos, gains], [tokens, perm, *weights], outs, scratch
+    )
 
 
 def room(count, channels):
@@ -288,7 +336,7 @@
     _, half, channels = arrays[0].shape
     count = 2 * (half // 72 - 1)
     outs = [(count * 72, channels)]
-    return call(early, "early", [], arrays, [gains], weights, 1, outs, room(count, channels))[0]
+    return call(early, "early", [], [*arrays, gains], weights, outs, room(count, channels))[0]
 
 
 def shifted_late(side, arrays, perm, gains, weights):
@@ -296,14 +344,19 @@
     count = 2 * (kept // 72 + 1)
     half = perm.shape[0]
     outs = [(2, 2, half // 2, channels)]
-    scratch = room(count, channels) + [pltpu.VMEM((half, channels), F32)]
-    return call(late, "late", [side], arrays, [perm, gains], weights, 1, outs, scratch)[0]
+    scratch = room(count, channels) + [
+        pltpu.VMEM((half, channels), F32),
+        pltpu.VMEM(outs[0], BF),
+        pltpu.VMEM(perm.shape, BF),
+    ]
+    far = [perm, *weights]
+    return call(late, "late", [side], [*arrays, gains], far, outs, scratch, keep=False)[0]
 
 
 def shards(tokens, gains, w_qkv, w_proj, w_in, w_out):
     levels, height, breadth, channels = tokens.shape
     perm_a, perm_b, back = tables(breadth)
-    weights = (w_qkv, w_proj, w_in, w_out)
+    weights = [w_qkv, w_proj, w_in, w_out]
     lats, lons = lax.axis_size("lat"), lax.axis_size("lon")
     place = lax.axis_index("lat")
     side = (place % 2).astype(jnp.int32).reshape(1)

time: 81.5 us -> 68.9 us (0.85)
  Pallas kernels: 63.1 us -> 53.8 us
  local copies, waits for them, and re-layouts: 4.38 us -> 1.44 us
    pallas_call x4, Pallas kernels: 63.1 us -> 53.8 us  [call(): pl.pallas_call(body, in_specs=[pl.BlockSpec(memory_space=pltpu.SMEM) for...]
    unnamed x16 -> x6, local copies, waits for them, and re-layouts: 2.97 us -> 0.01 us
where the time goes in v2:
time: 68.9 us; the launch traced here: 68.7 us
  Pallas kernels  53.8 us (78%)
  starting transfers between devices  12.9 us (19%)
  local copies, waits for them, and re-layouts  1.44 us (2%)
    pallas_call x4, Pallas kernels, call(): pl.pallas_call(body, in_specs=[pl.BlockSpec(memory_space=pltpu.SMEM) for...  53.8 us
    ppermute x4, starting transfers between devices, swap(): return lax.ppermute(block, 'lat', route)  10.4 us
    ppermute x2, starting transfers between devices, beside(): return lax.ppermute(column(part), 'lon', route)  2.49 us
  transfers between devices with their start and end apart: 6, of which 0 were waited for; matrix products, arithmetic and copies ran while one was open for 1% of the time, Pallas kernels for 55%

profile of v2, /device:TPU:0, one launch (start us, length us, event | category | flops | bytes accessed | tf_op | source)
XLA Modules:
  0.0 68.7 jit_solution(10521326455847229774)
XLA Ops:
  0.0 0.0 copy-start
  0.0 1.1 %fusion = (bf16[2,12,6,512]{3,2,1,0:T(8,128)(2,1)S(1)}, bf16[2,12,6,512]{3,2,1,0:T(8,128)(2,1)S(1)}) fusion(bf16[2,12,48,512]{3,2,1,0:T(8,128)(2,1)} %param.11), kind=kLoop, calls=%fused_computation.3 | loop fusion | bytes 589824 | tf_op jit(solution)/shard_map/slice | solution.py:378
  1.1 0.2 copy.14
  1.3 2.4 %collective-permute-start.2 = (bf16[2,72,512]{2,1,0:T(8,128)(2,1)S(1)}, bf16[2,72,512]{2,1,0:T(8,128)(2,1)S(1)}, u32[]{:S(2)}, u32[]{:S(2)}) collective-permute-start(bf16[2,72,512]{2,1,0:T(8,128)(2,1)S(1)} %copy.15), channel_id=1, source_target_pairs={{1,0},{2,1},{3,2},{0,3},{5,4},{6,5},{7,6},{4,7},{9,8},{10,9},{11,1... | collective-permute-start | bytes 442376 | tf_op jit(solution)/shard_map/ppermute | solution.py:370
  3.7 0.2 copy.16
  3.9 0.1 collective-permute-start.3
  4.0 0.0 copy-done
  4.0 12.7 %regular_a.1 = (bf16[2,360,512]{2,1,0:T(8,128)(2,1)S(1)}, bf16[360,512]{1,0:T(8,128)(2,1)S(1)}, bf16[360,512]{1,0:T(8,128)(2,1)S(1)}) custom-call(s32[1]{0:T(128)} %bitcast.side_ref, f32[4,512]{1,0:T(4,128)S(1)} %copy-done, bf16[2,576,512]{2,1,0:T(8,128)(2,1)} %bitcast.13, bf16[360,576]{1,0:T(8,128)(2,1)} %constant.39.clone.refs_2_, ...), custom_call_target="tpu_custom_call" | custom-call | tf_op jit(solution)/shard_map/regular_a/pallas_call | solution.py:293
  16.7 0.9 %collective-permute-start = (bf16[360,512]{1,0:T(8,128)(2,1)S(1)}, bf16[360,512]{1,0:T(8,128)(2,1)S(1)}, u32[]{:S(2)}, u32[]{:S(2)}) collective-permute-start(bf16[360,512]{1,0:T(8,128)(2,1)S(1)} %get-tuple-element.12.cross_ref.ca_ref), channel_id=1, source_target_pairs={{4,8},{8,4},{12,16},{16,12},{20,24},{24,20},{5,9},{9,5},{13,17},{1... | collective-permute-start | bytes 1105928 | tf_op jit(solution)/shard_map/ppermute | solution.py:376
  17.6 4.3 %collective-permute-start.1 = (bf16[360,512]{1,0:T(8,128)(2,1)S(1)}, bf16[360,512]{1,0:T(8,128)(2,1)S(1)}, u32[]{:S(2)}, u32[]{:S(2)}) collective-permute-start(bf16[360,512]{1,0:T(8,128)(2,1)S(1)} %get-tuple-element.13.same_ref.sa_ref), channel_id=1, source_target_pairs={{0,4},{4,0},{8,12},{12,8},{16,20},{20,16},{24,28},{28,24},{1,5},{5... | collective-permute-start | bytes 1105928 | tf_op jit(solution)/shard_map/ppermute | solution.py:376
  21.9 0.1 compare_or_fusion
  22.0 0.0 copy-start.2
  22.0 0.0 copy-start.1
  22.0 0.0 collective-permute-done.2.refs_0_
  22.0 0.0 collective-permute-done.3.refs_1_
  22.0 12.6 %regular_b.1 = (bf16[2,288,512]{2,1,0:T(8,128)(2,1)S(1)}, bf16[288,512]{1,0:T(8,128)(2,1)S(1)}, bf16[288,512]{1,0:T(8,128)(2,1)S(1)}) custom-call(s32[1]{0:T(128)} %bitcast.side_ref, bf16[2,72,512]{2,1,0:T(8,128)(2,1)S(1)} %collective-permute-done.2.refs_0_, bf16[2,72,512]{2,1,0:T(8,128)(2,1)S(1)} %collective-permute-done.3.refs_1_, f32[4,512]{1,0:T(4,128)S(1)} %copy-done, ...), custom_call_target="tpu_custom_call" | custom-call | tf_op jit(solution)/shard_map/regular_b/pallas_call | solution.py:293
  34.7 0.9 %collective-permute-start.4 = (bf16[288,512]{1,0:T(8,128)(2,1)S(1)}, bf16[288,512]{1,0:T(8,128)(2,1)S(1)}, u32[]{:S(2)}, u32[]{:S(2)}) collective-permute-start(bf16[288,512]{1,0:T(8,128)(2,1)S(1)} %get-tuple-element.15.cb_ref), channel_id=1, source_target_pairs={{4,8},{8,4},{12,16},{16,12},{20,24},{24,20},{5,9},{9,5},{13,17},{1... | collective-permute-start | bytes 884744 | tf_op jit(solution)/shard_map/ppermute | solution.py:376
  35.6 4.3 %collective-permute-start.5 = (bf16[288,512]{1,0:T(8,128)(2,1)S(1)}, bf16[288,512]{1,0:T(8,128)(2,1)S(1)}, u32[]{:S(2)}, u32[]{:S(2)}) collective-permute-start(bf16[288,512]{1,0:T(8,128)(2,1)S(1)} %get-tuple-element.16.sb_ref), channel_id=1, source_target_pairs={{0,4},{4,0},{8,12},{12,8},{16,20},{20,16},{24,28},{28,24},{1,5},{5... | collective-permute-start | bytes 884744 | tf_op jit(solution)/shard_map/ppermute | solution.py:376
  39.9 0.0 copy-done.2
  39.9 0.1 and_not_fusion
  40.0 0.0 copy-done.1
  40.0 0.0 collective-permute-done.far_cross_ref.fca_ref
  40.0 0.0 collective-permute-done.1.far_same_ref.fsa_ref
  40.1 12.4 %early.1.done_ref = bf16[576,512]{1,0:T(8,128)(2,1)S(1)} custom-call(bf16[2,360,512]{2,1,0:T(8,128)(2,1)S(1)} %get-tuple-element.11.x_ref.xa_ref, bf16[360,512]{1,0:T(8,128)(2,1)S(1)} %get-tuple-element.12.cross_ref.ca_ref, bf16[360,512]{1,0:T(8,128)(2,1)S(1)} %get-tuple-element.13.same_ref.sa_ref, ...), custom_call_target="tpu_custom_call" | custom-call | tf_op jit(solution)/shard_map/early/pallas_call | solution.py:293
  52.4 0.0 collective-permute-done.4.fcb_ref
  52.4 0.0 collective-permute-done.5.fsb_ref
  52.4 16.1 %late.1 = bf16[2,2,288,512]{3,2,1,0:T(8,128)(2,1)} custom-call(s32[1]{0:T(128)} %bitcast.side_ref, bf16[576,512]{1,0:T(8,128)(2,1)S(1)} %early.1.done_ref, bf16[2,360,512]{2,1,0:T(8,128)(2,1)S(1)} %get-tuple-element.11.x_ref.xa_ref, bf16[2,288,512]{2,1,0:T(8,128)(2,1)S(1)} %get-tuple-element.14.xb_ref, ...), custom_call_target="tpu_custom_call" | custom-call | tf_op jit(solution)/shard_map/late/pallas_call | solution.py:293
  (3 shorter events, 0.1 us)
Async XLA Ops:
  0.0 4.0 %copy-start = (f32[4,512]{1,0:T(4,128)S(1)}, f32[4,512]{1,0:T(4,128)}, u32[]{:S(2)}) copy-start(f32[4,512]{1,0:T(4,128)} %gains_ref.3) | copy-start | bytes 24580
  1.3 20.7 %collective-permute-start.2 = (bf16[2,72,512]{2,1,0:T(8,128)(2,1)S(1)}, bf16[2,72,512]{2,1,0:T(8,128)(2,1)S(1)}, u32[]{:S(2)}, u32[]{:S(2)}) collective-permute-start(bf16[2,72,512]{2,1,0:T(8,128)(2,1)S(1)} %copy.15), channel_id=1, source_target_pairs={{1,0},{2,1},{3,2},{0,3},{5,4},{6,5},{7,6},{4,7},{9,8},{10,9},{11,1... | collective-permute-start | bytes 442376 | tf_op jit(solution)/shard_map/ppermute | solution.py:370
  3.9 18.1 %collective-permute-start.3 = (bf16[2,72,512]{2,1,0:T(8,128)(2,1)S(1)}, bf16[2,72,512]{2,1,0:T(8,128)(2,1)S(1)}, u32[]{:S(2)}, u32[]{:S(2)}) collective-permute-start(bf16[2,72,512]{2,1,0:T(8,128)(2,1)S(1)} %copy.17), channel_id=1, source_target_pairs={{3,0},{0,1},{1,2},{2,3},{7,4},{4,5},{5,6},{6,7},{11,8},{8,9},{9,10... | collective-permute-start | bytes 442376 | tf_op jit(solution)/shard_map/ppermute | solution.py:370
  16.7 23.3 %collective-permute-start = (bf16[360,512]{1,0:T(8,128)(2,1)S(1)}, bf16[360,512]{1,0:T(8,128)(2,1)S(1)}, u32[]{:S(2)}, u32[]{:S(2)}) collective-permute-start(bf16[360,512]{1,0:T(8,128)(2,1)S(1)} %get-tuple-element.12.cross_ref.ca_ref), channel_id=1, source_target_pairs={{4,8},{8,4},{12,16},{16,12},{20,24},{24,20},{5,9},{9,5},{13,17},{1... | collective-permute-start | bytes 1105928 | tf_op jit(solution)/shard_map/ppermute | solution.py:376
  17.6 22.5 %collective-permute-start.1 = (bf16[360,512]{1,0:T(8,128)(2,1)S(1)}, bf16[360,512]{1,0:T(8,128)(2,1)S(1)}, u32[]{:S(2)}, u32[]{:S(2)}) collective-permute-start(bf16[360,512]{1,0:T(8,128)(2,1)S(1)} %get-tuple-element.13.same_ref.sa_ref), channel_id=1, source_target_pairs={{0,4},{4,0},{8,12},{12,8},{16,20},{20,16},{24,28},{28,24},{1,5},{5... | collective-permute-start | bytes 1105928 | tf_op jit(solution)/shard_map/ppermute | solution.py:376
  22.0 17.9 %copy-start.2 = (pred[144]{0:T(512)(128)(4,1)S(1)}, pred[144]{0:T(512)(128)(4,1)}, u32[]{:S(2)}) copy-start(pred[144]{0:T(512)(128)(4,1)} %constant.46) | copy-start | bytes 436
  22.0 18.0 %copy-start.1 = (pred[72,144]{1,0:T(8,128)(4,1)S(1)}, pred[72,144]{1,0:T(8,128)(4,1)}, u32[]{:S(2)}) copy-start(pred[72,144]{1,0:T(8,128)(4,1)} %constant.45) | copy-start | bytes 31108
  34.7 17.7 %collective-permute-start.4 = (bf16[288,512]{1,0:T(8,128)(2,1)S(1)}, bf16[288,512]{1,0:T(8,128)(2,1)S(1)}, u32[]{:S(2)}, u32[]{:S(2)}) collective-permute-start(bf16[288,512]{1,0:T(8,128)(2,1)S(1)} %get-tuple-element.15.cb_ref), channel_id=1, source_target_pairs={{4,8},{8,4},{12,16},{16,12},{20,24},{24,20},{5,9},{9,5},{13,17},{1... | collective-permute-start | bytes 884744 | tf_op jit(solution)/shard_map/ppermute | solution.py:376
  35.6 16.8 %collective-permute-start.5 = (bf16[288,512]{1,0:T(8,128)(2,1)S(1)}, bf16[288,512]{1,0:T(8,128)(2,1)S(1)}, u32[]{:S(2)}, u32[]{:S(2)}) collective-permute-start(bf16[288,512]{1,0:T(8,128)(2,1)S(1)} %get-tuple-element.16.sb_ref), channel_id=1, source_target_pairs={{0,4},{4,0},{8,12},{12,8},{16,20},{20,16},{24,28},{28,24},{1,5},{5... | collective-permute-start | bytes 884744 | tf_op jit(solution)/shard_map/ppermute | solution.py:376

commit v3 on v2

--- a/solution.py
+++ b/solution.py
@@ -20,7 +20,7 @@
 F32 = jnp.float32
 UNIT = 36
 WIDTH0 = 128
-WIDTH1 = 256
+WIDTH1 = 128
 EXP_SCALE = float(32.0 ** -0.5 * np.log2(np.e))
 
 
@@ -129,7 +129,7 @@
         att[at] = attend(q, k, v, None, WIDTH0).astype(BF)
         return 0
 
-    lax.fori_loop(0, strips, window, 0)
+    lax.fori_loop(0, strips, window, 0, unroll=True)
     for copy in copies[5:]:
         copy.wait()
     new = finish(xs[...], att[...], gains_ref[1:2], wproj_ref[...], win_ref[...], wout_ref[...])
@@ -161,7 +161,7 @@
         kv[at] = dot(lhs[at], wqkv_ref[:, channels:]).astype(BF)
         return 0
 
-    lax.fori_loop(0, 2, project, 0)
+    lax.fori_loop(0, 2, project, 0, unroll=True)
 
     def window(i, _):
         at = pl.ds(pl.multiple_of(i * 144, 16), 144)
@@ -169,7 +169,7 @@
         os[i] = attend(qs[i], kv[at, :channels], kv[at, channels:], bias, WIDTH1)
         return 0
 
-    lax.fori_loop(0, count, window, 0)
+    lax.fori_loop(0, count, window, 0, unroll=True)
 
 
 def early(x_ref, cross_ref, same_ref, far_cross_ref, far_same_ref, bias_ref,

time: 68.9 us -> 61.3 us (0.89)
  Pallas kernels: 53.8 us -> 39.9 us
  waiting for transfers between devices: 0.02 us -> 6.43 us
    pallas_call x4, Pallas kernels: 53.8 us -> 39.9 us  [call(): pl.pallas_call(body, in_specs=[pl.BlockSpec(memory_space=pltpu.SMEM) for...]
    ppermute x4, waiting for transfers between devices: 0.01 us -> 6.42 us  [swap(): return lax.ppermute(block, 'lat', route)]
  transfers between devices with their start and end apart: 6 -> 6, of which waited for: 0 -> 1; matrix products, arithmetic and copies ran while one was open for 1% -> 1% of each run, Pallas kernels for 55% -> 47%
where the time goes in v3:
time: 61.3 us; the launch traced here: 61.2 us
  Pallas kernels  39.9 us (65%)
  starting transfers between devices  12.9 us (21%)
  waiting for transfers between devices  6.43 us (10%)
  local copies, waits for them, and re-layouts  1.44 us (2%)
    pallas_call x4, Pallas kernels, call(): pl.pallas_call(body, in_specs=[pl.BlockSpec(memory_space=pltpu.SMEM) for...  39.9 us
    ppermute x4, starting transfers between devices, swap(): return lax.ppermute(block, 'lat', route)  10.4 us
    ppermute x4, waiting for transfers between devices, swap(): return lax.ppermute(block, 'lat', route)  6.42 us
    ppermute x2, starting transfers between devices, beside(): return lax.ppermute(column(part), 'lon', route)  2.49 us
  transfers between devices with their start and end apart: 6, of which 1 were waited for; matrix products, arithmetic and copies ran while one was open for 1% of the time, Pallas kernels for 47%

profile of v3, /device:TPU:0, one launch (start us, length us, event | category | flops | bytes accessed | tf_op | source)
XLA Modules:
  0.0 61.2 jit_solution(6488500689366568357)
XLA Ops:
  0.0 0.0 copy-start
  0.0 1.1 %fusion = (bf16[2,12,6,512]{3,2,1,0:T(8,128)(2,1)S(1)}, bf16[2,12,6,512]{3,2,1,0:T(8,128)(2,1)S(1)}) fusion(bf16[2,12,48,512]{3,2,1,0:T(8,128)(2,1)} %param.11), kind=kLoop, calls=%fused_computation.3 | loop fusion | bytes 589824 | tf_op jit(solution)/shard_map/slice | solution.py:378
  1.1 0.2 copy.14
  1.3 2.4 %collective-permute-start.2 = (bf16[2,72,512]{2,1,0:T(8,128)(2,1)S(1)}, bf16[2,72,512]{2,1,0:T(8,128)(2,1)S(1)}, u32[]{:S(2)}, u32[]{:S(2)}) collective-permute-start(bf16[2,72,512]{2,1,0:T(8,128)(2,1)S(1)} %copy.15), channel_id=1, source_target_pairs={{1,0},{2,1},{3,2},{0,3},{5,4},{6,5},{7,6},{4,7},{9,8},{10,9},{11,1... | collective-permute-start | bytes 442376 | tf_op jit(solution)/shard_map/ppermute | solution.py:370
  3.7 0.2 copy.16
  3.9 0.1 collective-permute-start.3
  4.0 0.0 copy-done
  4.0 10.3 %regular_a.1 = (bf16[2,360,512]{2,1,0:T(8,128)(2,1)S(1)}, bf16[360,512]{1,0:T(8,128)(2,1)S(1)}, bf16[360,512]{1,0:T(8,128)(2,1)S(1)}) custom-call(s32[1]{0:T(128)} %bitcast.side_ref, f32[4,512]{1,0:T(4,128)S(1)} %copy-done, bf16[2,576,512]{2,1,0:T(8,128)(2,1)} %bitcast.13, bf16[360,576]{1,0:T(8,128)(2,1)} %constant.39.clone.refs_2_, ...), custom_call_target="tpu_custom_call" | custom-call | tf_op jit(solution)/shard_map/regular_a/pallas_call | solution.py:293
  14.2 0.9 %collective-permute-start = (bf16[360,512]{1,0:T(8,128)(2,1)S(1)}, bf16[360,512]{1,0:T(8,128)(2,1)S(1)}, u32[]{:S(2)}, u32[]{:S(2)}) collective-permute-start(bf16[360,512]{1,0:T(8,128)(2,1)S(1)} %get-tuple-element.12.cross_ref.ca_ref), channel_id=1, source_target_pairs={{4,8},{8,4},{12,16},{16,12},{20,24},{24,20},{5,9},{9,5},{13,17},{1... | collective-permute-start | bytes 1105928 | tf_op jit(solution)/shard_map/ppermute | solution.py:376
  15.1 4.3 %collective-permute-start.1 = (bf16[360,512]{1,0:T(8,128)(2,1)S(1)}, bf16[360,512]{1,0:T(8,128)(2,1)S(1)}, u32[]{:S(2)}, u32[]{:S(2)}) collective-permute-start(bf16[360,512]{1,0:T(8,128)(2,1)S(1)} %get-tuple-element.13.same_ref.sa_ref), channel_id=1, source_target_pairs={{0,4},{4,0},{8,12},{12,8},{16,20},{20,16},{24,28},{28,24},{1,5},{5... | collective-permute-start | bytes 1105928 | tf_op jit(solution)/shard_map/ppermute | solution.py:376
  19.5 0.1 compare_or_fusion
  19.5 0.0 copy-start.2
  19.5 0.0 copy-start.1
  19.5 0.0 collective-permute-done.2.refs_0_
  19.5 0.0 collective-permute-done.3.refs_1_
  19.6 10.2 %regular_b.1 = (bf16[2,288,512]{2,1,0:T(8,128)(2,1)S(1)}, bf16[288,512]{1,0:T(8,128)(2,1)S(1)}, bf16[288,512]{1,0:T(8,128)(2,1)S(1)}) custom-call(s32[1]{0:T(128)} %bitcast.side_ref, bf16[2,72,512]{2,1,0:T(8,128)(2,1)S(1)} %collective-permute-done.2.refs_0_, bf16[2,72,512]{2,1,0:T(8,128)(2,1)S(1)} %collective-permute-done.3.refs_1_, f32[4,512]{1,0:T(4,128)S(1)} %copy-done, ...), custom_call_target="tpu_custom_call" | custom-call | tf_op jit(solution)/shard_map/regular_b/pallas_call | solution.py:293
  29.7 0.9 %collective-permute-start.4 = (bf16[288,512]{1,0:T(8,128)(2,1)S(1)}, bf16[288,512]{1,0:T(8,128)(2,1)S(1)}, u32[]{:S(2)}, u32[]{:S(2)}) collective-permute-start(bf16[288,512]{1,0:T(8,128)(2,1)S(1)} %get-tuple-element.15.cb_ref), channel_id=1, source_target_pairs={{4,8},{8,4},{12,16},{16,12},{20,24},{24,20},{5,9},{9,5},{13,17},{1... | collective-permute-start | bytes 884744 | tf_op jit(solution)/shard_map/ppermute | solution.py:376
  30.6 4.3 %collective-permute-start.5 = (bf16[288,512]{1,0:T(8,128)(2,1)S(1)}, bf16[288,512]{1,0:T(8,128)(2,1)S(1)}, u32[]{:S(2)}, u32[]{:S(2)}) collective-permute-start(bf16[288,512]{1,0:T(8,128)(2,1)S(1)} %get-tuple-element.16.sb_ref), channel_id=1, source_target_pairs={{0,4},{4,0},{8,12},{12,8},{16,20},{20,16},{24,28},{28,24},{1,5},{5... | collective-permute-start | bytes 884744 | tf_op jit(solution)/shard_map/ppermute | solution.py:376
  35.0 0.0 copy-done.2
  35.0 0.1 and_not_fusion
  35.0 0.0 copy-done.1
  35.1 0.0 collective-permute-done.far_cross_ref.fca_ref
  35.1 6.4 %collective-permute-done.1.far_same_ref.fsa_ref = bf16[360,512]{1,0:T(8,128)(2,1)S(1)} collective-permute-done((bf16[360,512]{1,0:T(8,128)(2,1)S(1)}, bf16[360,512]{1,0:T(8,128)(2,1)S(1)}, u32[]{:S(2)}, u32[]{:S(2)}) %collective-permute-start.1) | collective-permute-done | bytes 368672 | tf_op jit(solution)/shard_map/ppermute | solution.py:376
  41.5 8.2 %early.1.done_ref = bf16[576,512]{1,0:T(8,128)(2,1)S(1)} custom-call(bf16[2,360,512]{2,1,0:T(8,128)(2,1)S(1)} %get-tuple-element.11.x_ref.xa_ref, bf16[360,512]{1,0:T(8,128)(2,1)S(1)} %get-tuple-element.12.cross_ref.ca_ref, bf16[360,512]{1,0:T(8,128)(2,1)S(1)} %get-tuple-element.13.same_ref.sa_ref, ...), custom_call_target="tpu_custom_call" | custom-call | tf_op jit(solution)/shard_map/early/pallas_call | solution.py:293
  49.7 0.0 collective-permute-done.4.fcb_ref
  49.7 0.0 collective-permute-done.5.fsb_ref
  49.8 11.2 %late.1 = bf16[2,2,288,512]{3,2,1,0:T(8,128)(2,1)} custom-call(s32[1]{0:T(128)} %bitcast.side_ref, bf16[576,512]{1,0:T(8,128)(2,1)S(1)} %early.1.done_ref, bf16[2,360,512]{2,1,0:T(8,128)(2,1)S(1)} %get-tuple-element.11.x_ref.xa_ref, bf16[2,288,512]{2,1,0:T(8,128)(2,1)S(1)} %get-tuple-element.14.xb_ref, ...), custom_call_target="tpu_custom_call" | custom-call | tf_op jit(solution)/shard_map/late/pallas_call | solution.py:293
  (3 shorter events, 0.1 us)
Async XLA Ops:
  0.0 4.0 %copy-start = (f32[4,512]{1,0:T(4,128)S(1)}, f32[4,512]{1,0:T(4,128)}, u32[]{:S(2)}) copy-start(f32[4,512]{1,0:T(4,128)} %gains_ref.3) | copy-start | bytes 24580
  1.3 18.3 %collective-permute-start.2 = (bf16[2,72,512]{2,1,0:T(8,128)(2,1)S(1)}, bf16[2,72,512]{2,1,0:T(8,128)(2,1)S(1)}, u32[]{:S(2)}, u32[]{:S(2)}) collective-permute-start(bf16[2,72,512]{2,1,0:T(8,128)(2,1)S(1)} %copy.15), channel_id=1, source_target_pairs={{1,0},{2,1},{3,2},{0,3},{5,4},{6,5},{7,6},{4,7},{9,8},{10,9},{11,1... | collective-permute-start | bytes 442376 | tf_op jit(solution)/shard_map/ppermute | solution.py:370
  3.9 15.7 %collective-permute-start.3 = (bf16[2,72,512]{2,1,0:T(8,128)(2,1)S(1)}, bf16[2,72,512]{2,1,0:T(8,128)(2,1)S(1)}, u32[]{:S(2)}, u32[]{:S(2)}) collective-permute-start(bf16[2,72,512]{2,1,0:T(8,128)(2,1)S(1)} %copy.17), channel_id=1, source_target_pairs={{3,0},{0,1},{1,2},{2,3},{7,4},{4,5},{5,6},{6,7},{11,8},{8,9},{9,10... | collective-permute-start | bytes 442376 | tf_op jit(solution)/shard_map/ppermute | solution.py:370
  14.2 20.8 %collective-permute-start = (bf16[360,512]{1,0:T(8,128)(2,1)S(1)}, bf16[360,512]{1,0:T(8,128)(2,1)S(1)}, u32[]{:S(2)}, u32[]{:S(2)}) collective-permute-start(bf16[360,512]{1,0:T(8,128)(2,1)S(1)} %get-tuple-element.12.cross_ref.ca_ref), channel_id=1, source_target_pairs={{4,8},{8,4},{12,16},{16,12},{20,24},{24,20},{5,9},{9,5},{13,17},{1... | collective-permute-start | bytes 1105928 | tf_op jit(solution)/shard_map/ppermute | solution.py:376
  15.1 26.4 %collective-permute-start.1 = (bf16[360,512]{1,0:T(8,128)(2,1)S(1)}, bf16[360,512]{1,0:T(8,128)(2,1)S(1)}, u32[]{:S(2)}, u32[]{:S(2)}) collective-permute-start(bf16[360,512]{1,0:T(8,128)(2,1)S(1)} %get-tuple-element.13.same_ref.sa_ref), channel_id=1, source_target_pairs={{0,4},{4,0},{8,12},{12,8},{16,20},{20,16},{24,28},{28,24},{1,5},{5... | collective-permute-start | bytes 1105928 | tf_op jit(solution)/shard_map/ppermute | solution.py:376
  19.5 15.4 %copy-start.2 = (pred[144]{0:T(512)(128)(4,1)S(1)}, pred[144]{0:T(512)(128)(4,1)}, u32[]{:S(2)}) copy-start(pred[144]{0:T(512)(128)(4,1)} %constant.46) | copy-start | bytes 436
  19.5 15.5 %copy-start.1 = (pred[72,144]{1,0:T(8,128)(4,1)S(1)}, pred[72,144]{1,0:T(8,128)(4,1)}, u32[]{:S(2)}) copy-start(pred[72,144]{1,0:T(8,128)(4,1)} %constant.45) | copy-start | bytes 31108
  29.7 20.0 %collective-permute-start.4 = (bf16[288,512]{1,0:T(8,128)(2,1)S(1)}, bf16[288,512]{1,0:T(8,128)(2,1)S(1)}, u32[]{:S(2)}, u32[]{:S(2)}) collective-permute-start(bf16[288,512]{1,0:T(8,128)(2,1)S(1)} %get-tuple-element.15.cb_ref), channel_id=1, source_target_pairs={{4,8},{8,4},{12,16},{16,12},{20,24},{24,20},{5,9},{9,5},{13,17},{1... | collective-permute-start | bytes 884744 | tf_op jit(solution)/shard_map/ppermute | solution.py:376
  30.6 19.1 %collective-permute-start.5 = (bf16[288,512]{1,0:T(8,128)(2,1)S(1)}, bf16[288,512]{1,0:T(8,128)(2,1)S(1)}, u32[]{:S(2)}, u32[]{:S(2)}) collective-permute-start(bf16[288,512]{1,0:T(8,128)(2,1)S(1)} %get-tuple-element.16.sb_ref), channel_id=1, source_target_pairs={{0,4},{4,0},{8,12},{12,8},{16,20},{20,16},{24,28},{28,24},{1,5},{5... | collective-permute-start | bytes 884744 | tf_op jit(solution)/shard_map/ppermute | solution.py:376

commit v4 on v3

--- a/solution.py
+++ b/solution.py
@@ -91,8 +91,8 @@
     ]
 
 
-def block0(keep, side_ref, *refs):
-    *halos, gains_ref, x_far, perm_far, wqkv_far, wproj_far, win_far, wout_far = refs[:-14]
+def block0(side_ref, *refs):
+    gains_ref, x_far, perm_far, wqkv_far, wproj_far, win_far, wout_far = refs[:-14]
     x1_ref, cross_ref, same_ref, xs, qkv, att, xf, x_ref, perm_ref = refs[-14:-5]
     wqkv_ref, wproj_ref, win_ref, wout_ref, sems = refs[-5:]
     moves = [(perm_far, perm_ref), (x_far.at[0], x_ref.at[0]), (x_far.at[1], x_ref.at[1])]
@@ -109,10 +109,6 @@
     parts = []
     for r in range(2):
         nat = [x_ref[z, quarter * r : quarter * (r + 1)] for z in range(2)]
-        if halos:
-            nat.append(
-                jnp.concatenate([h[r].astype(F32) for h in halos], axis=0).astype(BF)
-            )
         nat = jnp.concatenate(nat, axis=0)
         parts.append(dot(perm, nat).reshape(strips, 72, channels))
     x = jnp.concatenate(parts, axis=1).reshape(tokens, channels)
@@ -139,8 +135,8 @@
     odd = side_ref[0]
     for g, n_ref in ((0, cross_ref), (1, same_ref)):
         mine = pltpu.roll(xf[jnp.where(odd == 0, g, 1 - g)], UNIT, 0).astype(BF)
-        x1_ref[g] = mine[:keep]
-        n_ref[...] = norm(mine.astype(F32), gains_ref[2:3])[:keep]
+        x1_ref[g] = mine
+        n_ref[...] = norm(mine.astype(F32), gains_ref[2:3])
 
 
 def blocks(rows):
@@ -179,15 +175,19 @@
     rooms = (wqkv_ref, wproj_ref, win_ref, wout_ref)
     copies = fetch(weight_moves((wqkv_far, wproj_far, win_far, wout_far), rooms, 1), sems)
 
+    def inner(rows):
+        part = blocks(rows)
+        return [part[1:2], part[3:4]]
+
     def pair(a_ref, b_ref):
-        return jnp.concatenate([blocks(a_ref[...])[1:], blocks(b_ref[...])[1:]], axis=0)
+        return jnp.concatenate(inner(a_ref[...]) + inner(b_ref[...]), axis=0)
 
     own, far = pair(cross_ref, same_ref), pair(far_cross_ref, far_same_ref)
     windows(own, far, bias_ref, wqkv_ref, copies[:2], lhs, qs, kv, os)
     for copy in copies[2:]:
         copy.wait()
     rows = own.shape[0] * 72
-    x = jnp.concatenate([blocks(x_ref[g])[1:] for g in range(2)], axis=0).reshape(rows, channels)
+    x = jnp.concatenate(inner(x_ref[0]) + inner(x_ref[1]), axis=0).reshape(rows, channels)
     attended = os[...].reshape(rows, channels).astype(BF)
     out_ref[...] = finish(
         x, attended, gains_ref[3:4], wproj_ref[...], win_ref[...], wout_ref[...]
@@ -195,7 +195,7 @@
 
 
 def late(side_ref, done_ref, xa_ref, xb_ref, ca_ref, sa_ref, cb_ref, sb_ref,
-         fca_ref, fsa_ref, fcb_ref, fsb_ref, bias_ref,
+         fca_ref, fsa_ref, fcb_ref, fsb_ref, left_ref, right_ref, bias_ref,
          gains_ref, perm_far, wqkv_far, wproj_far, win_far, wout_far,
          out_far, lhs, qs, kv, os, tile_ref, out_ref, perm_ref,
          wqkv_ref, wproj_ref, win_ref, wout_ref, sems):
@@ -205,17 +205,19 @@
     copies = fetch(moves + [(perm_far, perm_ref)], sems)
     first = lax.broadcasted_iota(jnp.int32, (72, channels), 0) < UNIT
 
-    def extend(a, b):
-        a, b = blocks(a), blocks(b)
-        mid, lead = jnp.where(first, a[0], b[0]), jnp.where(first, b[0], a[0])
-        return jnp.concatenate([mid[None], b[1:], lead[None]], axis=0)
-
-    own = jnp.concatenate(
-        [extend(ca_ref[...], cb_ref[...]), extend(sa_ref[...], sb_ref[...])], axis=0
-    )
-    far = jnp.concatenate(
-        [extend(fca_ref[...], fcb_ref[...]), extend(fsa_ref[...], fsb_ref[...])], axis=0
-    )
+    def inside(a, b):
+        near_side = jnp.where(first, a[0], b[0])
+        far_side = jnp.where(first, b[0], a[0])
+        return [near_side[None], b[1:], far_side[None]]
+
+    def extend(a_ref, b_ref, index):
+        a, b = blocks(a_ref[...]), blocks(b_ref[...])
+        lead = jnp.where(first, left_ref[index].astype(F32), a[2])
+        tail = jnp.where(first, a[2], right_ref[index].astype(F32))
+        return inside(a, b) + [lead[None], tail[None]]
+
+    own = jnp.concatenate(extend(ca_ref, cb_ref, 0) + extend(sa_ref, sb_ref, 1), axis=0)
+    far = jnp.concatenate(extend(fca_ref, fcb_ref, 2) + extend(fsa_ref, fsb_ref, 3), axis=0)
     windows(own, far, bias_ref, wqkv_ref, copies[:2], lhs, qs, kv, os)
     for copy in copies[2:]:
         copy.wait()
@@ -225,24 +227,20 @@
     for g in range(2):
         a, b = blocks(xa_ref[g]), blocks(xb_ref[g])
         o = os[count * g : count * (g + 1)]
-        xs += [
-            jnp.where(first, b[last], a[0])[None],
-            jnp.where(first, a[0], b[0])[None],
-            b[1:last],
-        ]
-        atts += [jnp.where(first, o[last], o[count - 1])[None], o[:last]]
+        xs += [a[2:3]] + inside(a, b)
+        atts += [jnp.where(first, o[last + 1], o[last])[None], o[:last]]
     rows = (count - 1) * 72
     x = jnp.concatenate(xs, axis=0).reshape(2 * rows, channels)
     attended = jnp.concatenate(atts, axis=0).reshape(2 * rows, channels).astype(BF)
     new = finish(x, attended, gains_ref[3:4], wproj_ref[...], win_ref[...], wout_ref[...])
     ready = done_ref[...].astype(F32)
-    share = ready.shape[0] // 2
     odd = side_ref[0]
     sent = []
     for g in range(2):
         tile_ref[:72] = new[rows * g : rows * g + 72]
-        tile_ref[72 : 72 + share] = ready[share * g : share * (g + 1)]
-        tile_ref[72 + share :] = new[rows * g + 72 : rows * (g + 1)]
+        tile_ref[72:144] = ready[144 * g + 72 : 144 * (g + 1)]
+        tile_ref[144 : 72 + rows] = new[rows * g + 72 : rows * (g + 1)]
+        tile_ref[72 + rows :] = ready[144 * g : 144 * g + 72]
         nat = dot(perm_ref[...], tile_ref[...].astype(BF)).astype(BF)
         quarter = nat.shape[0] // 2
         r = jnp.where(odd == 0, g, 1 - g)
@@ -273,14 +271,8 @@
     half = order.size
     onehot = np.zeros((half, half), np.float32)
     onehot[np.arange(half), order] = 1.0
-    cut = 72 * (strips // 2 + 1)
-    halo = np.zeros((72, 72), np.float32)
-    halo[np.arange(72), orders(1)] = 1.0
-    rest = np.zeros((half - cut + 144, half + 144), np.float32)
-    rest[: half - cut, :half] = onehot[cut:]
-    rest[half - cut : half - cut + 72, half : half + 72] = halo
-    rest[half - cut + 72 :, half + 72 :] = halo
-    made = (onehot[:cut], rest, np.roll(onehot, UNIT, axis=0).T)
+    outer = np.concatenate([onehot[half - 144 :], onehot[:144]])
+    made = (outer, onehot[144 : half - 144], np.roll(onehot, UNIT, axis=0).T)
     return tuple(jnp.asarray(m, BF) for m in made)
 
 
@@ -303,11 +295,10 @@
     )(*scalars, *[near(a) for a in arrays], *[pltpu.with_memory_space_constraint(a, pltpu.HBM) for a in far])
 
 
-def regular(side, tokens, halos, perm, gains, weights):
+def regular(name, side, tokens, perm, gains, weights):
     channels = tokens.shape[-1]
     half = perm.shape[0]
-    keep = half - 72 if halos else half
-    outs = [(2, keep, channels), (keep, channels), (keep, channels)]
+    outs = [(2, half, channels), (half, channels), (half, channels)]
     scratch = [
         pltpu.VMEM((2 * half, channels), BF),
         pltpu.VMEM((2 * half, 3 * channels), BF),
@@ -316,11 +307,7 @@
         pltpu.VMEM(tokens.shape, BF),
         pltpu.VMEM(perm.shape, BF),
     ]
-    body = functools.partial(block0, keep)
-    name = "regular_b" if halos else "regular_a"
-    return call(
-        body, name, [side], [*halos, gains], [tokens, perm, *weights], outs, scratch
-    )
+    return call(block0, name, [side], [gains], [tokens, perm, *weights], outs, scratch)
 
 
 def room(count, channels):
@@ -333,15 +320,15 @@
 
 
 def shifted_early(arrays, gains, weights):
-    _, half, channels = arrays[0].shape
-    count = 2 * (half // 72 - 1)
+    channels = arrays[0].shape[-1]
+    count = 4
     outs = [(count * 72, channels)]
     return call(early, "early", [], [*arrays, gains], weights, outs, room(count, channels))[0]
 
 
 def shifted_late(side, arrays, perm, gains, weights):
     _, kept, channels = arrays[2].shape
-    count = 2 * (kept // 72 + 1)
+    count = 2 * (kept // 72 + 3)
     half = perm.shape[0]
     outs = [(2, 2, half // 2, channels)]
     scratch = room(count, channels) + [
@@ -354,20 +341,16 @@
 
 
 def shards(tokens, gains, w_qkv, w_proj, w_in, w_out):
-    levels, height, breadth, channels = tokens.shape
-    perm_a, perm_b, back = tables(breadth)
+    breadth, channels = tokens.shape[2:]
+    outer, inner, back = tables(breadth)
     weights = [w_qkv, w_proj, w_in, w_out]
     lats, lons = lax.axis_size("lat"), lax.axis_size("lon")
     place = lax.axis_index("lat")
     side = (place % 2).astype(jnp.int32).reshape(1)
 
-    def column(part):
-        part = part.reshape(levels, 2, SY, WX, channels).transpose(1, 0, 2, 3, 4)
-        return part.reshape(2, 72, channels)
-
     def beside(part, distance):
         route = [((x + distance) % lons, x) for x in range(lons)]
-        return lax.ppermute(column(part), "lon", route)
+        return lax.ppermute(part, "lon", route)
 
     def swap(block, first):
         route = []
@@ -375,13 +358,13 @@
             route += [(y, y + 1), (y + 1, y)]
         return lax.ppermute(block, "lat", route)
 
-    left = beside(tokens[:, :, breadth - WX :], -1)
-    right = beside(tokens[:, :, :WX], 1)
     tile = tokens.reshape(2, -1, channels)
-    xa, ca, sa = regular(side, tile, [], perm_a, gains, weights)
+    xa, ca, sa = regular("outer", side, tile, outer, gains, weights)
     fca, fsa = swap(ca, 1), swap(sa, 0)
-    xb, cb, sb = regular(side, tile, [right, left], perm_b, gains, weights)
+    xb, cb, sb = regular("inner", side, tile, inner, gains, weights)
     fcb, fsb = swap(cb, 1), swap(sb, 0)
+    edge = jnp.stack([part[144:216] for part in (ca, sa, fca, fsa)])
+    left, right = beside(edge, -1), beside(edge, 1)
 
     token = np.arange(72)
     lev = token % UNIT // (UNIT // 2)
@@ -393,9 +376,8 @@
     allowed = same[None] & ~(dead[:, None, None] & far[None, None, :])
     bias = jnp.where(allowed, 0.0, NEGATIVE).astype(F32)
     done = shifted_early([xa, ca, sa, fca, fsa, bias], gains, weights)
-    out = shifted_late(
-        side, [done, xa, xb, ca, sa, cb, sb, fca, fsa, fcb, fsb, bias], back, gains, weights
-    )
+    arrays = [done, xa, xb, ca, sa, cb, sb, fca, fsa, fcb, fsb, left, right, bias]
+    out = shifted_late(side, arrays, back, gains, weights)
     return out.reshape(tokens.shape)
 
 

time: 61.3 us -> 57.8 us (0.943)
  Pallas kernels: 39.9 us -> 36.6 us
  other arithmetic: 0.17 us -> 0.94 us
  local copies, waits for them, and re-layouts: 1.44 us -> 0.73 us
  starting transfers between devices: 12.9 us -> 12.2 us
    pallas_call x4, Pallas kernels: 39.9 us -> 36.6 us  [call(): pl.pallas_call(body, in_specs=[pl.BlockSpec(memory_space=pltpu.SMEM) for...]
    ppermute x2, waiting for transfers between devices: 0.01 us -> 2.72 us  [beside(): return lax.ppermute(part, 'lon', route)]
    ppermute x4, waiting for transfers between devices: 6.42 us -> 4.14 us  [swap(): return lax.ppermute(block, 'lat', route)]
    ppermute x2, starting transfers between devices: 2.49 us -> 0.55 us  [beside(): return lax.ppermute(part, 'lon', route)]
    ppermute x4, starting transfers between devices: 10.4 us -> 11.7 us  [swap(): return lax.ppermute(block, 'lat', route)]
    slice x1 -> x0, local copies, waits for them, and re-layouts: 1.08 us -> none  [shards(): left = beside(tokens[:, :, breadth - WX:], -1)]
    select_n x1, other arithmetic: 0.02 us -> 0.74 us  [shards(): bias = jnp.where(allowed, 0.0, NEGATIVE).astype(F32)]
    unnamed x6, local copies, waits for them, and re-layouts: 0.01 us -> 0.71 us
  transfers between devices with their start and end apart: 6 -> 6, of which waited for: 1 -> 2; matrix products, arithmetic and copies ran while one was open for 1% -> 2% of each run, Pallas kernels for 47% -> 24%
where the time goes in v4:
time: 57.8 us; the launch traced here: 57.6 us
  Pallas kernels  36.6 us (63%)
  starting transfers between devices  12.2 us (21%)
  waiting for transfers between devices  6.86 us (12%)
  other arithmetic  0.94 us (2%)
  local copies, waits for them, and re-layouts  0.73 us (1%)
    pallas_call x4, Pallas kernels, call(): pl.pallas_call(body, in_specs=[pl.BlockSpec(memory_space=pltpu.SMEM) for...  36.6 us
    ppermute x4, starting transfers between devices, swap(): return lax.ppermute(block, 'lat', route)  11.7 us
    ppermute x4, waiting for transfers between devices, swap(): return lax.ppermute(block, 'lat', route)  4.14 us
    ppermute x2, waiting for transfers between devices, beside(): return lax.ppermute(part, 'lon', route)  2.72 us
  transfers between devices with their start and end apart: 6, of which 2 were waited for; matrix products, arithmetic and copies ran while one was open for 2% of the time, Pallas kernels for 24%

profile of v4, /device:TPU:0, one launch (start us, length us, event | category | flops | bytes accessed | tf_op | source)
XLA Modules:
  0.0 57.6 jit_solution(5967383504469253745)
XLA Ops:
  0.0 0.0 copy-start
  0.0 0.7 %copy-done = f32[4,512]{1,0:T(4,128)S(1)} copy-done((f32[4,512]{1,0:T(4,128)S(1)}, f32[4,512]{1,0:T(4,128)}, u32[]{:S(2)}) %copy-start) | copy-done | bytes 8216
  0.7 8.8 %outer.1 = (bf16[2,288,512]{2,1,0:T(8,128)(2,1)S(1)}, bf16[288,512]{1,0:T(8,128)(2,1)S(1)}, bf16[288,512]{1,0:T(8,128)(2,1)S(1)}) custom-call(s32[1]{0:T(128)} %bitcast.side_ref, f32[4,512]{1,0:T(4,128)S(1)} %copy-done, bf16[2,576,512]{2,1,0:T(8,128)(2,1)} %bitcast.13, bf16[288,576]{1,0:T(8,128)(2,1)} %constant.39.clone.refs_2_, ...), custom_call_target="tpu_custom_call" | custom-call | tf_op jit(solution)/shard_map/outer/pallas_call | solution.py:285
  9.5 0.9 %collective-permute-start = (bf16[288,512]{1,0:T(8,128)(2,1)S(1)}, bf16[288,512]{1,0:T(8,128)(2,1)S(1)}, u32[]{:S(2)}, u32[]{:S(2)}) collective-permute-start(bf16[288,512]{1,0:T(8,128)(2,1)S(1)} %get-tuple-element.12.cross_ref.ca_ref), channel_id=1, source_target_pairs={{4,8},{8,4},{12,16},{16,12},{20,24},{24,20},{5,9},{9,5},{13,17},{1... | collective-permute-start | bytes 884744 | tf_op jit(solution)/shard_map/ppermute | solution.py:359
  10.3 0.0 copy-start.2
  10.3 0.0 copy-start.1
  10.4 5.8 %collective-permute-start.1 = (bf16[288,512]{1,0:T(8,128)(2,1)S(1)}, bf16[288,512]{1,0:T(8,128)(2,1)S(1)}, u32[]{:S(2)}, u32[]{:S(2)}) collective-permute-start(bf16[288,512]{1,0:T(8,128)(2,1)S(1)} %get-tuple-element.13.same_ref.sa_ref), channel_id=1, source_target_pairs={{0,4},{4,0},{8,12},{12,8},{16,20},{20,16},{24,28},{28,24},{1,5},{5... | collective-permute-start | bytes 884744 | tf_op jit(solution)/shard_map/ppermute | solution.py:359
  16.1 8.8 %inner.1 = (bf16[2,288,512]{2,1,0:T(8,128)(2,1)S(1)}, bf16[288,512]{1,0:T(8,128)(2,1)S(1)}, bf16[288,512]{1,0:T(8,128)(2,1)S(1)}) custom-call(s32[1]{0:T(128)} %bitcast.side_ref, f32[4,512]{1,0:T(4,128)S(1)} %copy-done, bf16[2,576,512]{2,1,0:T(8,128)(2,1)} %bitcast.14, bf16[288,576]{1,0:T(8,128)(2,1)} %constant.40.clone.refs_2_, ...), custom_call_target="tpu_custom_call" | custom-call | tf_op jit(solution)/shard_map/inner/pallas_call | solution.py:285
  24.9 0.7 %collective-permute-start.2 = (bf16[288,512]{1,0:T(8,128)(2,1)S(1)}, bf16[288,512]{1,0:T(8,128)(2,1)S(1)}, u32[]{:S(2)}, u32[]{:S(2)}) collective-permute-start(bf16[288,512]{1,0:T(8,128)(2,1)S(1)} %get-tuple-element.15.cb_ref), channel_id=1, source_target_pairs={{4,8},{8,4},{12,16},{16,12},{20,24},{24,20},{5,9},{9,5},{13,17},{1... | collective-permute-start | bytes 884744 | tf_op jit(solution)/shard_map/ppermute | solution.py:359
  25.6 4.3 %collective-permute-start.3 = (bf16[288,512]{1,0:T(8,128)(2,1)S(1)}, bf16[288,512]{1,0:T(8,128)(2,1)S(1)}, u32[]{:S(2)}, u32[]{:S(2)}) collective-permute-start(bf16[288,512]{1,0:T(8,128)(2,1)S(1)} %get-tuple-element.16.sb_ref), channel_id=1, source_target_pairs={{0,4},{4,0},{8,12},{12,8},{16,20},{20,16},{24,28},{28,24},{1,5},{5... | collective-permute-start | bytes 884744 | tf_op jit(solution)/shard_map/ppermute | solution.py:359
  29.9 0.1 compare_or_fusion
  30.0 0.0 collective-permute-done.far_cross_ref.fca_ref
  30.0 4.1 %collective-permute-done.1.far_same_ref.fsa_ref = bf16[288,512]{1,0:T(8,128)(2,1)S(1)} collective-permute-done((bf16[288,512]{1,0:T(8,128)(2,1)S(1)}, bf16[288,512]{1,0:T(8,128)(2,1)S(1)}, u32[]{:S(2)}, u32[]{:S(2)}) %collective-permute-start.1) | collective-permute-done | bytes 294944 | tf_op jit(solution)/shard_map/ppermute | solution.py:359
  34.2 0.1 collective-permute-start.5
  34.3 0.5 collective-permute-start.4
  34.8 0.0 copy-done.2
  34.8 0.1 and_not_fusion
  34.9 0.7 %and_select_fusion.bias_ref = f32[2,72,144]{2,1,0:T(8,128)S(1)} fusion(pred[2,144]{1,0:T(4,128)(4,1)S(1)} %and_not_fusion, pred[72,144]{1,0:T(8,128)(4,1)} %constant.45), kind=kLoop, calls=%fused_computation.1 | loop fusion | flops 41472 | bytes 93600 | tf_op jit(solution)/shard_map/jit(_where)/select_n | solution.py:377
  35.6 0.0 copy-done.1
  35.6 5.3 %early.1.done_ref = bf16[288,512]{1,0:T(8,128)(2,1)S(1)} custom-call(bf16[2,288,512]{2,1,0:T(8,128)(2,1)S(1)} %get-tuple-element.11.x_ref.xa_ref, bf16[288,512]{1,0:T(8,128)(2,1)S(1)} %get-tuple-element.12.cross_ref.ca_ref, bf16[288,512]{1,0:T(8,128)(2,1)S(1)} %get-tuple-element.13.same_ref.sa_ref, ...), custom_call_target="tpu_custom_call" | custom-call | tf_op jit(solution)/shard_map/early/pallas_call | solution.py:285
  40.9 0.0 collective-permute-done.2.fcb_ref
  40.9 0.0 collective-permute-done.3.fsb_ref
  40.9 0.0 collective-permute-done.5.right_ref
  40.9 2.7 %collective-permute-done.4.left_ref = bf16[4,72,512]{2,1,0:T(8,128)(2,1)S(1)} collective-permute-done((bf16[4,72,512]{2,1,0:T(8,128)(2,1)S(1)}, bf16[4,72,512]{2,1,0:T(8,128)(2,1)S(1)}, u32[]{:S(2)}, u32[]{:S(2)}) %collective-permute-start.4) | collective-permute-done | bytes 294944 | tf_op jit(solution)/shard_map/ppermute | solution.py:353
  43.6 13.8 %late.1 = bf16[2,2,288,512]{3,2,1,0:T(8,128)(2,1)} custom-call(s32[1]{0:T(128)} %bitcast.side_ref, bf16[288,512]{1,0:T(8,128)(2,1)S(1)} %early.1.done_ref, bf16[2,288,512]{2,1,0:T(8,128)(2,1)S(1)} %get-tuple-element.11.x_ref.xa_ref, bf16[2,288,512]{2,1,0:T(8,128)(2,1)S(1)} %get-tuple-element.14.xb_ref, ...), custom_call_target="tpu_custom_call" | custom-call | tf_op jit(solution)/shard_map/late/pallas_call | solution.py:285
  (4 shorter events, 0.1 us)
Async XLA Ops:
  0.0 0.7 %copy-start = (f32[4,512]{1,0:T(4,128)S(1)}, f32[4,512]{1,0:T(4,128)}, u32[]{:S(2)}) copy-start(f32[4,512]{1,0:T(4,128)} %gains_ref.3) | copy-start | bytes 24580
  9.5 20.6 %collective-permute-start = (bf16[288,512]{1,0:T(8,128)(2,1)S(1)}, bf16[288,512]{1,0:T(8,128)(2,1)S(1)}, u32[]{:S(2)}, u32[]{:S(2)}) collective-permute-start(bf16[288,512]{1,0:T(8,128)(2,1)S(1)} %get-tuple-element.12.cross_ref.ca_ref), channel_id=1, source_target_pairs={{4,8},{8,4},{12,16},{16,12},{20,24},{24,20},{5,9},{9,5},{13,17},{1... | collective-permute-start | bytes 884744 | tf_op jit(solution)/shard_map/ppermute | solution.py:359
  10.3 24.5 %copy-start.2 = (pred[144]{0:T(512)(128)(4,1)S(1)}, pred[144]{0:T(512)(128)(4,1)}, u32[]{:S(2)}) copy-start(pred[144]{0:T(512)(128)(4,1)} %constant.46) | copy-start | bytes 436
  10.3 25.3 %copy-start.1 = (f32[4,512]{1,0:T(4,128)S(1)}, f32[4,512]{1,0:T(4,128)}, u32[]{:S(2)}) copy-start(f32[4,512]{1,0:T(4,128)} %gains_ref.3) | copy-start | bytes 24580
  10.4 23.8 %collective-permute-start.1 = (bf16[288,512]{1,0:T(8,128)(2,1)S(1)}, bf16[288,512]{1,0:T(8,128)(2,1)S(1)}, u32[]{:S(2)}, u32[]{:S(2)}) collective-permute-start(bf16[288,512]{1,0:T(8,128)(2,1)S(1)} %get-tuple-element.13.same_ref.sa_ref), channel_id=1, source_target_pairs={{0,4},{4,0},{8,12},{12,8},{16,20},{20,16},{24,28},{28,24},{1,5},{5... | collective-permute-start | bytes 884744 | tf_op jit(solution)/shard_map/ppermute | solution.py:359
  24.9 16.0 %collective-permute-start.2 = (bf16[288,512]{1,0:T(8,128)(2,1)S(1)}, bf16[288,512]{1,0:T(8,128)(2,1)S(1)}, u32[]{:S(2)}, u32[]{:S(2)}) collective-permute-start(bf16[288,512]{1,0:T(8,128)(2,1)S(1)} %get-tuple-element.15.cb_ref), channel_id=1, source_target_pairs={{4,8},{8,4},{12,16},{16,12},{20,24},{24,20},{5,9},{9,5},{13,17},{1... | collective-permute-start | bytes 884744 | tf_op jit(solution)/shard_map/ppermute | solution.py:359
  25.6 15.3 %collective-permute-start.3 = (bf16[288,512]{1,0:T(8,128)(2,1)S(1)}, bf16[288,512]{1,0:T(8,128)(2,1)S(1)}, u32[]{:S(2)}, u32[]{:S(2)}) collective-permute-start(bf16[288,512]{1,0:T(8,128)(2,1)S(1)} %get-tuple-element.16.sb_ref), channel_id=1, source_target_pairs={{0,4},{4,0},{8,12},{12,8},{16,20},{20,16},{24,28},{28,24},{1,5},{5... | collective-permute-start | bytes 884744 | tf_op jit(solution)/shard_map/ppermute | solution.py:359
  34.2 6.7 %collective-permute-start.5 = (bf16[4,72,512]{2,1,0:T(8,128)(2,1)S(1)}, bf16[4,72,512]{2,1,0:T(8,128)(2,1)S(1)}, u32[]{:S(2)}, u32[]{:S(2)}) collective-permute-start(bf16[4,72,512]{2,1,0:T(8,128)(2,1)S(1)} %pad_maximum_fusion), channel_id=1, source_target_pairs={{1,0},{2,1},{3,2},{0,3},{5,4},{6,5},{7,6},{4,7},{9,8},{10,9},{11,1... | collective-permute-start | bytes 884744 | tf_op jit(solution)/shard_map/ppermute | solution.py:353
  34.3 9.3 %collective-permute-start.4 = (bf16[4,72,512]{2,1,0:T(8,128)(2,1)S(1)}, bf16[4,72,512]{2,1,0:T(8,128)(2,1)S(1)}, u32[]{:S(2)}, u32[]{:S(2)}) collective-permute-start(bf16[4,72,512]{2,1,0:T(8,128)(2,1)S(1)} %pad_maximum_fusion), channel_id=1, source_target_pairs={{3,0},{0,1},{1,2},{2,3},{7,4},{4,5},{5,6},{6,7},{11,8},{8,9},{9,10... | collective-permute-start | bytes 884744 | tf_op jit(solution)/shard_map/ppermute | solution.py:353

commit v5 on v4

--- a/solution.py
+++ b/solution.py
@@ -92,10 +92,11 @@
 
 
 def block0(side_ref, *refs):
-    gains_ref, x_far, perm_far, wqkv_far, wproj_far, win_far, wout_far = refs[:-14]
-    x1_ref, cross_ref, same_ref, xs, qkv, att, xf, x_ref, perm_ref = refs[-14:-5]
-    wqkv_ref, wproj_ref, win_ref, wout_ref, sems = refs[-5:]
-    moves = [(perm_far, perm_ref), (x_far.at[0], x_ref.at[0]), (x_far.at[1], x_ref.at[1])]
+    gains_far, x_far, perm_far, wqkv_far, wproj_far, win_far, wout_far = refs[:-15]
+    x1_ref, cross_ref, same_ref, xs, qkv, att, xf, x_ref, perm_ref = refs[-15:-6]
+    gains_ref, wqkv_ref, wproj_ref, win_ref, wout_ref, sems = refs[-6:]
+    moves = [(gains_far, gains_ref), (perm_far, perm_ref)]
+    moves += [(x_far.at[z], x_ref.at[z]) for z in range(2)]
     rooms = (wqkv_ref, wproj_ref, win_ref, wout_ref)
     moves += weight_moves((wqkv_far, wproj_far, win_far, wout_far), rooms, 0)
     copies = fetch(moves, sems)
@@ -103,7 +104,7 @@
     half = tokens // 2
     strips = half // 72
     quarter = x_ref.shape[1] // 2
-    for copy in copies[:3]:
+    for copy in copies[:4]:
         copy.wait()
     perm = perm_ref[...]
     parts = []
@@ -114,7 +115,7 @@
     x = jnp.concatenate(parts, axis=1).reshape(tokens, channels)
     xs[...] = x.astype(BF)
     normed = norm(x, gains_ref[0:1])
-    for copy in copies[3:5]:
+    for copy in copies[4:6]:
         copy.wait()
     qkv[...] = dot(normed, wqkv_ref[...]).astype(BF)
 
@@ -126,7 +127,7 @@
         return 0
 
     lax.fori_loop(0, strips, window, 0, unroll=True)
-    for copy in copies[5:]:
+    for copy in copies[6:]:
         copy.wait()
     new = finish(xs[...], att[...], gains_ref[1:2], wproj_ref[...], win_ref[...], wout_ref[...])
     new = new.reshape(strips, 2, 72, channels)
@@ -173,7 +174,8 @@
           wqkv_ref, wproj_ref, win_ref, wout_ref, sems):
     channels = x_ref.shape[-1]
     rooms = (wqkv_ref, wproj_ref, win_ref, wout_ref)
-    copies = fetch(weight_moves((wqkv_far, wproj_far, win_far, wout_far), rooms, 1), sems)
+    moves = weight_moves((wqkv_far, wproj_far, win_far, wout_far), rooms, 1)
+    copies = fetch(moves, sems)
 
     def inner(rows):
         part = blocks(rows)
@@ -279,26 +281,33 @@
 PARAMS = pltpu.CompilerParams(vmem_limit_bytes=LIMIT)
 
 
-def call(body, name, scalars, arrays, far, outs, scratch, keep=True):
+def call(body, name, scalars, arrays, far, weights, outs, scratch, keep=True):
+    far = [*far, *weights]
     vmem, hbm = (pl.BlockSpec(memory_space=m) for m in (pltpu.VMEM, pltpu.HBM))
-    weights = [pltpu.VMEM(w.shape[1:], BF) for w in far[-4:]]
+    space = pltpu.VMEM if keep else pltpu.HBM
+    kept = [pltpu.VMEM(w.shape[1:], BF) for w in weights]
     return pl.pallas_call(
         body,
         in_specs=[pl.BlockSpec(memory_space=pltpu.SMEM) for _ in scalars]
         + [vmem for _ in arrays]
         + [hbm for _ in far],
         out_specs=[vmem if keep else hbm for _ in outs],
-        out_shape=[pltpu.VMEM(o, BF) if keep else pltpu.HBM(o, BF) for o in outs],
-        scratch_shapes=scratch + weights + [pltpu.SemaphoreType.DMA((8,))],
+        out_shape=[space(*o) for o in outs],
+        scratch_shapes=scratch + kept + [pltpu.SemaphoreType.DMA((10,))],
         compiler_params=PARAMS,
         name=name,
-    )(*scalars, *[near(a) for a in arrays], *[pltpu.with_memory_space_constraint(a, pltpu.HBM) for a in far])
-
-
-def regular(name, side, tokens, perm, gains, weights):
+    )(
+        *scalars,
+        *[near(a) for a in arrays],
+        *[pltpu.with_memory_space_constraint(a, pltpu.HBM) for a in far],
+    )
+
+
+def regular(name, scalars, tokens, perm, gains, weights):
     channels = tokens.shape[-1]
     half = perm.shape[0]
-    outs = [(2, half, channels), (half, channels), (half, channels)]
+    shapes = [(2, half, channels), (half, channels), (half, channels)]
+    outs = [(shape, BF) for shape in shapes]
     scratch = [
         pltpu.VMEM((2 * half, channels), BF),
         pltpu.VMEM((2 * half, 3 * channels), BF),
@@ -306,8 +315,9 @@
         pltpu.VMEM((2, half, channels), F32),
         pltpu.VMEM(tokens.shape, BF),
         pltpu.VMEM(perm.shape, BF),
+        pltpu.VMEM(gains.shape, F32),
     ]
-    return call(block0, name, [side], [gains], [tokens, perm, *weights], outs, scratch)
+    return call(block0, name, scalars, [], [gains, tokens, perm], weights, outs, scratch)
 
 
 def room(count, channels):
@@ -322,22 +332,22 @@
 def shifted_early(arrays, gains, weights):
     channels = arrays[0].shape[-1]
     count = 4
-    outs = [(count * 72, channels)]
-    return call(early, "early", [], [*arrays, gains], weights, outs, room(count, channels))[0]
+    outs = [((count * 72, channels), BF)]
+    return call(early, "early", [], [*arrays, gains], [], weights, outs, room(count, channels))[0]
 
 
 def shifted_late(side, arrays, perm, gains, weights):
     _, kept, channels = arrays[2].shape
     count = 2 * (kept // 72 + 3)
     half = perm.shape[0]
-    outs = [(2, 2, half // 2, channels)]
+    shape = (2, 2, half // 2, channels)
     scratch = room(count, channels) + [
         pltpu.VMEM((half, channels), F32),
-        pltpu.VMEM(outs[0], BF),
+        pltpu.VMEM(shape, BF),
         pltpu.VMEM(perm.shape, BF),
     ]
-    far = [perm, *weights]
-    return call(late, "late", [side], [*arrays, gains], far, outs, scratch, keep=False)[0]
+    arrays, outs = [*arrays, gains], [(shape, BF)]
+    return call(late, "late", [side], arrays, [perm], weights, outs, scratch, keep=False)[0]
 
 
 def shards(tokens, gains, w_qkv, w_proj, w_in, w_out):
@@ -358,23 +368,25 @@
             route += [(y, y + 1), (y + 1, y)]
         return lax.ppermute(block, "lat", route)
 
+    step = 1 - 2 * (place % 2)
+    partners = jnp.stack([place - step, place + step])
+    dead = (partners < 0) | (partners >= lats)
+    token = np.arange(72)
+    lev = token % UNIT // (UNIT // 2)
+    same = np.tile(lev[:, None] == lev[None, :], (1, 2))
+    live = np.stack([same, same & (np.arange(144) < 72)])
+    table = jnp.asarray(np.where(live, 0.0, NEGATIVE), F32)
+    bias = jnp.where(dead[:, None, None], table[1], table[0])
+
     tile = tokens.reshape(2, -1, channels)
-    xa, ca, sa = regular("outer", side, tile, outer, gains, weights)
+    xa, ca, sa = regular("outer", [side], tile, outer, gains, weights)
     fca, fsa = swap(ca, 1), swap(sa, 0)
-    xb, cb, sb = regular("inner", side, tile, inner, gains, weights)
+    xb, cb, sb = regular("inner", [side], tile, inner, gains, weights)
+    sb, bias = lax.optimization_barrier((sb, bias))
     fcb, fsb = swap(cb, 1), swap(sb, 0)
     edge = jnp.stack([part[144:216] for part in (ca, sa, fca, fsa)])
     left, right = beside(edge, -1), beside(edge, 1)
 
-    token = np.arange(72)
-    lev = token % UNIT // (UNIT // 2)
-    same = np.tile(lev[:, None] == lev[None, :], (1, 2))
-    far = np.arange(144) >= 72
-    step = 1 - 2 * (place % 2)
-    partners = jnp.stack([place - step, place + step])
-    dead = (partners < 0) | (partners >= lats)
-    allowed = same[None] & ~(dead[:, None, None] & far[None, None, :])
-    bias = jnp.where(allowed, 0.0, NEGATIVE).astype(F32)
     done = shifted_early([xa, ca, sa, fca, fsa, bias], gains, weights)
     arrays = [done, xa, xb, ca, sa, cb, sb, fca, fsa, fcb, fsb, left, right, bias]
     out = shifted_late(side, arrays, back, gains, weights)

time: 57.8 us -> 54.1 us (0.936)
  starting transfers between devices: 12.2 us -> 8.46 us
  waiting for transfers between devices: 6.86 us -> 8.14 us
  other arithmetic: 0.94 us -> 0.2 us
  local copies, waits for them, and re-layouts: 0.73 us -> 0.04 us
    ppermute x4, starting transfers between devices: 11.7 us -> 7.39 us  [swap(): return lax.ppermute(block, 'lat', route)]
    ppermute x4, waiting for transfers between devices: 4.14 us -> 8.13 us  [swap(): return lax.ppermute(block, 'lat', route)]
    ppermute x2, waiting for transfers between devices: 2.72 us -> 0.01 us  [beside(): return lax.ppermute(part, 'lon', route)]
    unnamed x6, local copies, waits for them, and re-layouts: 0.71 us -> 0.01 us
    select_n x1, other arithmetic: 0.74 us -> 0.08 us  [shards(): bias = jnp.where(dead[:, None, None], table[1], table[0])]
  transfers between devices with their start and end apart: 6 -> 6, of which waited for: 2 -> 2; matrix products, arithmetic and copies ran while one was open for 2% -> 0% of each run, Pallas kernels for 24% -> 26%
where the time goes in v5:
time: 54.1 us; the launch traced here: 54 us
  Pallas kernels  36.9 us (68%)
  starting transfers between devices  8.46 us (16%)
  waiting for transfers between devices  8.14 us (15%)
    pallas_call x4, Pallas kernels, call(): pl.pallas_call(body, in_specs=[pl.BlockSpec(memory_space=pltpu.SMEM) for...  36.9 us
    ppermute x4, waiting for transfers between devices, swap(): return lax.ppermute(block, 'lat', route)  8.13 us
    ppermute x4, starting transfers between devices, swap(): return lax.ppermute(block, 'lat', route)  7.39 us
  transfers between devices with their start and end apart: 6, of which 2 were waited for; matrix products, arithmetic and copies ran while one was open for 0% of the time, Pallas kernels for 26%

profile of v5, /device:TPU:0, one launch (start us, length us, event | category | flops | bytes accessed | tf_op | source)
XLA Modules:
  0.0 54.0 jit_solution(4792958897874894478)
XLA Ops:
  0.0 0.0 copy-start.1
  0.0 0.0 copy-start.2
  0.0 8.8 %outer.1 = (bf16[2,288,512]{2,1,0:T(8,128)(2,1)S(1)}, bf16[288,512]{1,0:T(8,128)(2,1)S(1)}, bf16[288,512]{1,0:T(8,128)(2,1)S(1)}) custom-call(s32[1]{0:T(128)} %bitcast.side_ref, f32[4,512]{1,0:T(4,128)} %gains_ref.3, bf16[2,576,512]{2,1,0:T(8,128)(2,1)} %bitcast.13, bf16[288,576]{1,0:T(8,128)(2,1)} %constant.33.clone.refs_2_, ...), custom_call_target="tpu_custom_call" | custom-call | tf_op jit(solution)/shard_map/outer/pallas_call | solution.py:289
  8.9 0.9 %collective-permute-start = (bf16[288,512]{1,0:T(8,128)(2,1)S(1)}, bf16[288,512]{1,0:T(8,128)(2,1)S(1)}, u32[]{:S(2)}, u32[]{:S(2)}) collective-permute-start(bf16[288,512]{1,0:T(8,128)(2,1)S(1)} %get-tuple-element.14.cross_ref.ca_ref), channel_id=1, source_target_pairs={{4,8},{8,4},{12,16},{16,12},{20,24},{24,20},{5,9},{9,5},{13,17},{1... | collective-permute-start | bytes 884744 | tf_op jit(solution)/shard_map/ppermute | solution.py:369
  9.7 5.8 %collective-permute-start.1 = (bf16[288,512]{1,0:T(8,128)(2,1)S(1)}, bf16[288,512]{1,0:T(8,128)(2,1)S(1)}, u32[]{:S(2)}, u32[]{:S(2)}) collective-permute-start(bf16[288,512]{1,0:T(8,128)(2,1)S(1)} %get-tuple-element.15.same_ref.sa_ref), channel_id=1, source_target_pairs={{0,4},{4,0},{8,12},{12,8},{16,20},{20,16},{24,28},{28,24},{1,5},{5... | collective-permute-start | bytes 884744 | tf_op jit(solution)/shard_map/ppermute | solution.py:369
  15.5 0.1 compare_or_fusion
  15.6 0.0 copy-done.1
  15.6 0.0 copy-done.2
  15.6 0.1 broadcast_select_fusion.bias_ref
  15.7 0.0 copy-start
  15.7 8.8 %inner.1 = (bf16[2,288,512]{2,1,0:T(8,128)(2,1)S(1)}, bf16[288,512]{1,0:T(8,128)(2,1)S(1)}, bf16[288,512]{1,0:T(8,128)(2,1)S(1)}) custom-call(s32[1]{0:T(128)} %bitcast.side_ref, f32[4,512]{1,0:T(4,128)} %gains_ref.3, bf16[2,576,512]{2,1,0:T(8,128)(2,1)} %bitcast.14, bf16[288,576]{1,0:T(8,128)(2,1)} %constant.34.clone.refs_2_, ...), custom_call_target="tpu_custom_call" | custom-call | tf_op jit(solution)/shard_map/inner/pallas_call | solution.py:289
  24.5 0.1 collective-permute-start.3
  24.6 0.7 %collective-permute-start.2 = (bf16[288,512]{1,0:T(8,128)(2,1)S(1)}, bf16[288,512]{1,0:T(8,128)(2,1)S(1)}, u32[]{:S(2)}, u32[]{:S(2)}) collective-permute-start(bf16[288,512]{1,0:T(8,128)(2,1)S(1)} %get-tuple-element.19.cb_ref), channel_id=1, source_target_pairs={{4,8},{8,4},{12,16},{16,12},{20,24},{24,20},{5,9},{9,5},{13,17},{1... | collective-permute-start | bytes 884744 | tf_op jit(solution)/shard_map/ppermute | solution.py:369
  25.3 0.0 collective-permute-done.far_cross_ref.fca_ref
  25.3 2.0 %collective-permute-done.1.far_same_ref.fsa_ref = bf16[288,512]{1,0:T(8,128)(2,1)S(1)} collective-permute-done((bf16[288,512]{1,0:T(8,128)(2,1)S(1)}, bf16[288,512]{1,0:T(8,128)(2,1)S(1)}, u32[]{:S(2)}, u32[]{:S(2)}) %collective-permute-start.1) | collective-permute-done | bytes 294944 | tf_op jit(solution)/shard_map/ppermute | solution.py:369
  27.3 1.1 %collective-permute-start.5 = (bf16[4,72,512]{2,1,0:T(8,128)(2,1)S(1)}, bf16[4,72,512]{2,1,0:T(8,128)(2,1)S(1)}, u32[]{:S(2)}, u32[]{:S(2)}) collective-permute-start(bf16[4,72,512]{2,1,0:T(8,128)(2,1)S(1)} %pad_maximum_fusion), channel_id=1, source_target_pairs={{1,0},{2,1},{3,2},{0,3},{5,4},{6,5},{7,6},{4,7},{9,8},{10,9},{11,1... | collective-permute-start | bytes 884744 | tf_op jit(solution)/shard_map/ppermute | solution.py:363
  28.4 0.0 collective-permute-start.4
  28.4 0.0 copy-done
  28.4 5.3 %early.1.done_ref = bf16[288,512]{1,0:T(8,128)(2,1)S(1)} custom-call(bf16[2,288,512]{2,1,0:T(8,128)(2,1)S(1)} %get-tuple-element.13.x_ref.xa_ref, bf16[288,512]{1,0:T(8,128)(2,1)S(1)} %get-tuple-element.14.cross_ref.ca_ref, bf16[288,512]{1,0:T(8,128)(2,1)S(1)} %get-tuple-element.15.same_ref.sa_ref, ...), custom_call_target="tpu_custom_call" | custom-call | tf_op jit(solution)/shard_map/early/pallas_call | solution.py:289
  33.7 6.1 %collective-permute-done.3.fsb_ref = bf16[288,512]{1,0:T(8,128)(2,1)S(1)} collective-permute-done((bf16[288,512]{1,0:T(8,128)(2,1)S(1)}, bf16[288,512]{1,0:T(8,128)(2,1)S(1)}, u32[]{:S(2)}, u32[]{:S(2)}) %collective-permute-start.3) | collective-permute-done | bytes 294944 | tf_op jit(solution)/shard_map/ppermute | solution.py:369
  39.8 0.0 collective-permute-done.2.fcb_ref
  39.8 0.0 collective-permute-done.5.right_ref
  39.8 0.0 collective-permute-done.4.left_ref
  39.8 13.9 %late.1 = bf16[2,2,288,512]{3,2,1,0:T(8,128)(2,1)} custom-call(s32[1]{0:T(128)} %bitcast.side_ref, bf16[288,512]{1,0:T(8,128)(2,1)S(1)} %early.1.done_ref, bf16[2,288,512]{2,1,0:T(8,128)(2,1)S(1)} %get-tuple-element.13.x_ref.xa_ref, bf16[2,288,512]{2,1,0:T(8,128)(2,1)S(1)} %get-tuple-element.18.xb_ref, ...), custom_call_target="tpu_custom_call" | custom-call | tf_op jit(solution)/shard_map/late/pallas_call | solution.py:289
  (4 shorter events, 0.1 us)
Async XLA Ops:
  0.0 15.6 %copy-start.1 = (f32[72,144]{1,0:T(8,128)S(1)}, f32[72,144]{1,0:T(8,128)}, u32[]{:S(2)}) copy-start(f32[72,144]{1,0:T(8,128)} %constant.41) | copy-start | bytes 124420
  0.0 15.6 %copy-start.2 = (f32[72,144]{1,0:T(8,128)S(1)}, f32[72,144]{1,0:T(8,128)}, u32[]{:S(2)}) copy-start(f32[72,144]{1,0:T(8,128)} %constant.39) | copy-start | bytes 124420
  8.9 16.4 %collective-permute-start = (bf16[288,512]{1,0:T(8,128)(2,1)S(1)}, bf16[288,512]{1,0:T(8,128)(2,1)S(1)}, u32[]{:S(2)}, u32[]{:S(2)}) collective-permute-start(bf16[288,512]{1,0:T(8,128)(2,1)S(1)} %get-tuple-element.14.cross_ref.ca_ref), channel_id=1, source_target_pairs={{4,8},{8,4},{12,16},{16,12},{20,24},{24,20},{5,9},{9,5},{13,17},{1... | collective-permute-start | bytes 884744 | tf_op jit(solution)/shard_map/ppermute | solution.py:369
  9.7 17.6 %collective-permute-start.1 = (bf16[288,512]{1,0:T(8,128)(2,1)S(1)}, bf16[288,512]{1,0:T(8,128)(2,1)S(1)}, u32[]{:S(2)}, u32[]{:S(2)}) collective-permute-start(bf16[288,512]{1,0:T(8,128)(2,1)S(1)} %get-tuple-element.15.same_ref.sa_ref), channel_id=1, source_target_pairs={{0,4},{4,0},{8,12},{12,8},{16,20},{20,16},{24,28},{28,24},{1,5},{5... | collective-permute-start | bytes 884744 | tf_op jit(solution)/shard_map/ppermute | solution.py:369
  15.7 12.7 %copy-start = (f32[4,512]{1,0:T(4,128)S(1)}, f32[4,512]{1,0:T(4,128)}, u32[]{:S(2)}) copy-start(f32[4,512]{1,0:T(4,128)} %gains_ref.3) | copy-start | bytes 24580
  24.5 15.3 %collective-permute-start.3 = (bf16[288,512]{1,0:T(8,128)(2,1)S(1)}, bf16[288,512]{1,0:T(8,128)(2,1)S(1)}, u32[]{:S(2)}, u32[]{:S(2)}) collective-permute-start(bf16[288,512]{1,0:T(8,128)(2,1)S(1)} %get-tuple-element.20.sb_ref), channel_id=1, source_target_pairs={{0,4},{4,0},{8,12},{12,8},{16,20},{20,16},{24,28},{28,24},{1,5},{5... | collective-permute-start | bytes 884744 | tf_op jit(solution)/shard_map/ppermute | solution.py:369
  24.6 15.3 %collective-permute-start.2 = (bf16[288,512]{1,0:T(8,128)(2,1)S(1)}, bf16[288,512]{1,0:T(8,128)(2,1)S(1)}, u32[]{:S(2)}, u32[]{:S(2)}) collective-permute-start(bf16[288,512]{1,0:T(8,128)(2,1)S(1)} %get-tuple-element.19.cb_ref), channel_id=1, source_target_pairs={{4,8},{8,4},{12,16},{16,12},{20,24},{24,20},{5,9},{9,5},{13,17},{1... | collective-permute-start | bytes 884744 | tf_op jit(solution)/shard_map/ppermute | solution.py:369
  27.3 12.5 %collective-permute-start.5 = (bf16[4,72,512]{2,1,0:T(8,128)(2,1)S(1)}, bf16[4,72,512]{2,1,0:T(8,128)(2,1)S(1)}, u32[]{:S(2)}, u32[]{:S(2)}) collective-permute-start(bf16[4,72,512]{2,1,0:T(8,128)(2,1)S(1)} %pad_maximum_fusion), channel_id=1, source_target_pairs={{1,0},{2,1},{3,2},{0,3},{5,4},{6,5},{7,6},{4,7},{9,8},{10,9},{11,1... | collective-permute-start | bytes 884744 | tf_op jit(solution)/shard_map/ppermute | solution.py:363
  28.4 11.4 %collective-permute-start.4 = (bf16[4,72,512]{2,1,0:T(8,128)(2,1)S(1)}, bf16[4,72,512]{2,1,0:T(8,128)(2,1)S(1)}, u32[]{:S(2)}, u32[]{:S(2)}) collective-permute-start(bf16[4,72,512]{2,1,0:T(8,128)(2,1)S(1)} %pad_maximum_fusion), channel_id=1, source_target_pairs={{3,0},{0,1},{1,2},{2,3},{7,4},{4,5},{5,6},{6,7},{11,8},{8,9},{9,10... | collective-permute-start | bytes 884744 | tf_op jit(solution)/shard_map/ppermute | solution.py:363

commit v6 on v5

--- a/solution.py
+++ b/solution.py
@@ -198,12 +198,12 @@
 
 def late(side_ref, done_ref, xa_ref, xb_ref, ca_ref, sa_ref, cb_ref, sb_ref,
          fca_ref, fsa_ref, fcb_ref, fsb_ref, left_ref, right_ref, bias_ref,
-         gains_ref, perm_far, wqkv_far, wproj_far, win_far, wout_far,
+         gains_ref, wqkv_ref, perm_far, wproj_far, win_far, wout_far,
          out_far, lhs, qs, kv, os, tile_ref, out_ref, perm_ref,
-         wqkv_ref, wproj_ref, win_ref, wout_ref, sems):
+         wproj_ref, win_ref, wout_ref, sems):
     channels = xa_ref.shape[-1]
-    rooms = (wqkv_ref, wproj_ref, win_ref, wout_ref)
-    moves = weight_moves((wqkv_far, wproj_far, win_far, wout_far), rooms, 1)
+    pairs = ((wproj_far, wproj_ref), (win_far, win_ref), (wout_far, wout_ref))
+    moves = [(w.at[1], room) for w, room in pairs]
     copies = fetch(moves + [(perm_far, perm_ref)], sems)
     first = lax.broadcasted_iota(jnp.int32, (72, channels), 0) < UNIT
 
@@ -220,8 +220,8 @@
 
     own = jnp.concatenate(extend(ca_ref, cb_ref, 0) + extend(sa_ref, sb_ref, 1), axis=0)
     far = jnp.concatenate(extend(fca_ref, fcb_ref, 2) + extend(fsa_ref, fsb_ref, 3), axis=0)
-    windows(own, far, bias_ref, wqkv_ref, copies[:2], lhs, qs, kv, os)
-    for copy in copies[2:]:
+    windows(own, far, bias_ref, wqkv_ref.at[1], [], lhs, qs, kv, os)
+    for copy in copies:
         copy.wait()
     count = own.shape[0] // 2
     last = count - 2
@@ -346,8 +346,8 @@
         pltpu.VMEM(shape, BF),
         pltpu.VMEM(perm.shape, BF),
     ]
-    arrays, outs = [*arrays, gains], [(shape, BF)]
-    return call(late, "late", [side], arrays, [perm], weights, outs, scratch, keep=False)[0]
+    arrays, outs = [*arrays, gains, weights[0]], [(shape, BF)]
+    return call(late, "late", [side], arrays, [perm], weights[1:], outs, scratch, keep=False)[0]
 
 
 def shards(tokens, gains, w_qkv, w_proj, w_in, w_out):

time: 54.1 us -> 52.8 us (0.976)
  Pallas kernels: 36.9 us -> 35.7 us
    pallas_call x4, Pallas kernels: 36.9 us -> 35.7 us  [call(): pl.pallas_call(body, in_specs=[pl.BlockSpec(memory_space=pltpu.SMEM) for...]
  transfers between devices with their start and end apart: 6 -> 6, of which waited for: 2 -> 2; matrix products, arithmetic and copies ran while one was open for 0% -> 0% of each run, Pallas kernels for 26% -> 27%
where the time goes in v6:
time: 52.8 us; the launch traced here: 52.7 us
  Pallas kernels  35.7 us (68%)
  starting transfers between devices  8.46 us (16%)
  waiting for transfers between devices  7.96 us (15%)
    pallas_call x4, Pallas kernels, call(): pl.pallas_call(body, in_specs=[pl.BlockSpec(memory_space=pltpu.SMEM) for...  35.7 us
    ppermute x4, waiting for transfers between devices, swap(): return lax.ppermute(block, 'lat', route)  7.95 us
    ppermute x4, starting transfers between devices, swap(): return lax.ppermute(block, 'lat', route)  7.39 us
    ppermute x2, starting transfers between devices, beside(): return lax.ppermute(part, 'lon', route)  1.07 us
  transfers between devices with their start and end apart: 6, of which 2 were waited for; matrix products, arithmetic and copies ran while one was open for 0% of the time, Pallas kernels for 27%

profile of v6, /device:TPU:0, one launch (start us, length us, event | category | flops | bytes accessed | tf_op | source)
XLA Modules:
  0.0 52.7 jit_solution(14227232566216537587)
XLA Ops:
  0.0 0.0 copy-start.2
  0.0 0.0 copy-start.3
  0.0 8.8 %outer.1 = (bf16[2,288,512]{2,1,0:T(8,128)(2,1)S(1)}, bf16[288,512]{1,0:T(8,128)(2,1)S(1)}, bf16[288,512]{1,0:T(8,128)(2,1)S(1)}) custom-call(s32[1]{0:T(128)} %bitcast.side_ref, f32[4,512]{1,0:T(4,128)} %gains_ref.3, bf16[2,576,512]{2,1,0:T(8,128)(2,1)} %bitcast.13, bf16[288,576]{1,0:T(8,128)(2,1)} %constant.33.clone.refs_2_, ...), custom_call_target="tpu_custom_call" | custom-call | tf_op jit(solution)/shard_map/outer/pallas_call | solution.py:289
  8.9 0.9 %collective-permute-start = (bf16[288,512]{1,0:T(8,128)(2,1)S(1)}, bf16[288,512]{1,0:T(8,128)(2,1)S(1)}, u32[]{:S(2)}, u32[]{:S(2)}) collective-permute-start(bf16[288,512]{1,0:T(8,128)(2,1)S(1)} %get-tuple-element.14.cross_ref.ca_ref), channel_id=1, source_target_pairs={{4,8},{8,4},{12,16},{16,12},{20,24},{24,20},{5,9},{9,5},{13,17},{1... | collective-permute-start | bytes 884744 | tf_op jit(solution)/shard_map/ppermute | solution.py:369
  9.7 5.8 %collective-permute-start.1 = (bf16[288,512]{1,0:T(8,128)(2,1)S(1)}, bf16[288,512]{1,0:T(8,128)(2,1)S(1)}, u32[]{:S(2)}, u32[]{:S(2)}) collective-permute-start(bf16[288,512]{1,0:T(8,128)(2,1)S(1)} %get-tuple-element.15.same_ref.sa_ref), channel_id=1, source_target_pairs={{0,4},{4,0},{8,12},{12,8},{16,20},{20,16},{24,28},{28,24},{1,5},{5... | collective-permute-start | bytes 884744 | tf_op jit(solution)/shard_map/ppermute | solution.py:369
  15.5 0.1 compare_or_fusion
  15.6 0.0 copy-done.2
  15.6 0.0 copy-done.3
  15.6 0.1 broadcast_select_fusion.bias_ref
  15.7 0.0 copy-start.1
  15.7 8.8 %inner.1 = (bf16[2,288,512]{2,1,0:T(8,128)(2,1)S(1)}, bf16[288,512]{1,0:T(8,128)(2,1)S(1)}, bf16[288,512]{1,0:T(8,128)(2,1)S(1)}) custom-call(s32[1]{0:T(128)} %bitcast.side_ref, f32[4,512]{1,0:T(4,128)} %gains_ref.3, bf16[2,576,512]{2,1,0:T(8,128)(2,1)} %bitcast.14, bf16[288,576]{1,0:T(8,128)(2,1)} %constant.34.clone.refs_2_, ...), custom_call_target="tpu_custom_call" | custom-call | tf_op jit(solution)/shard_map/inner/pallas_call | solution.py:289
  24.5 0.1 collective-permute-start.3
  24.6 0.7 %collective-permute-start.2 = (bf16[288,512]{1,0:T(8,128)(2,1)S(1)}, bf16[288,512]{1,0:T(8,128)(2,1)S(1)}, u32[]{:S(2)}, u32[]{:S(2)}) collective-permute-start(bf16[288,512]{1,0:T(8,128)(2,1)S(1)} %get-tuple-element.19.cb_ref), channel_id=1, source_target_pairs={{4,8},{8,4},{12,16},{16,12},{20,24},{24,20},{5,9},{9,5},{13,17},{1... | collective-permute-start | bytes 884744 | tf_op jit(solution)/shard_map/ppermute | solution.py:369
  25.3 0.0 collective-permute-done.far_cross_ref.fca_ref
  25.3 2.0 %collective-permute-done.1.far_same_ref.fsa_ref = bf16[288,512]{1,0:T(8,128)(2,1)S(1)} collective-permute-done((bf16[288,512]{1,0:T(8,128)(2,1)S(1)}, bf16[288,512]{1,0:T(8,128)(2,1)S(1)}, u32[]{:S(2)}, u32[]{:S(2)}) %collective-permute-start.1) | collective-permute-done | bytes 294944 | tf_op jit(solution)/shard_map/ppermute | solution.py:369
  27.3 1.1 %collective-permute-start.5 = (bf16[4,72,512]{2,1,0:T(8,128)(2,1)S(1)}, bf16[4,72,512]{2,1,0:T(8,128)(2,1)S(1)}, u32[]{:S(2)}, u32[]{:S(2)}) collective-permute-start(bf16[4,72,512]{2,1,0:T(8,128)(2,1)S(1)} %pad_maximum_fusion), channel_id=1, source_target_pairs={{1,0},{2,1},{3,2},{0,3},{5,4},{6,5},{7,6},{4,7},{9,8},{10,9},{11,1... | collective-permute-start | bytes 884744 | tf_op jit(solution)/shard_map/ppermute | solution.py:363
  28.4 0.0 collective-permute-start.4
  28.4 0.0 copy-done.1
  28.4 0.0 copy-start
  28.4 5.4 %early.1.done_ref = bf16[288,512]{1,0:T(8,128)(2,1)S(1)} custom-call(bf16[2,288,512]{2,1,0:T(8,128)(2,1)S(1)} %get-tuple-element.13.x_ref.xa_ref, bf16[288,512]{1,0:T(8,128)(2,1)S(1)} %get-tuple-element.14.cross_ref.ca_ref, bf16[288,512]{1,0:T(8,128)(2,1)S(1)} %get-tuple-element.15.same_ref.sa_ref, ...), custom_call_target="tpu_custom_call" | custom-call | tf_op jit(solution)/shard_map/early/pallas_call | solution.py:289
  33.9 6.0 %collective-permute-done.3.fsb_ref = bf16[288,512]{1,0:T(8,128)(2,1)S(1)} collective-permute-done((bf16[288,512]{1,0:T(8,128)(2,1)S(1)}, bf16[288,512]{1,0:T(8,128)(2,1)S(1)}, u32[]{:S(2)}, u32[]{:S(2)}) %collective-permute-start.3) | collective-permute-done | bytes 294944 | tf_op jit(solution)/shard_map/ppermute | solution.py:369
  39.8 0.0 collective-permute-done.2.fcb_ref
  39.8 0.0 collective-permute-done.5.right_ref
  39.8 0.0 collective-permute-done.4.left_ref
  39.8 0.0 copy-done
  39.9 12.6 %late.1 = bf16[2,2,288,512]{3,2,1,0:T(8,128)(2,1)} custom-call(s32[1]{0:T(128)} %bitcast.side_ref, bf16[288,512]{1,0:T(8,128)(2,1)S(1)} %early.1.done_ref, bf16[2,288,512]{2,1,0:T(8,128)(2,1)S(1)} %get-tuple-element.13.x_ref.xa_ref, bf16[2,288,512]{2,1,0:T(8,128)(2,1)S(1)} %get-tuple-element.18.xb_ref, ...), custom_call_target="tpu_custom_call" | custom-call | tf_op jit(solution)/shard_map/late/pallas_call | solution.py:289
  (4 shorter events, 0.1 us)
Async XLA Ops:
  0.0 15.6 %copy-start.2 = (f32[72,144]{1,0:T(8,128)S(1)}, f32[72,144]{1,0:T(8,128)}, u32[]{:S(2)}) copy-start(f32[72,144]{1,0:T(8,128)} %constant.41) | copy-start | bytes 124420
  0.0 15.6 %copy-start.3 = (f32[72,144]{1,0:T(8,128)S(1)}, f32[72,144]{1,0:T(8,128)}, u32[]{:S(2)}) copy-start(f32[72,144]{1,0:T(8,128)} %constant.39) | copy-start | bytes 124420
  8.9 16.4 %collective-permute-start = (bf16[288,512]{1,0:T(8,128)(2,1)S(1)}, bf16[288,512]{1,0:T(8,128)(2,1)S(1)}, u32[]{:S(2)}, u32[]{:S(2)}) collective-permute-start(bf16[288,512]{1,0:T(8,128)(2,1)S(1)} %get-tuple-element.14.cross_ref.ca_ref), channel_id=1, source_target_pairs={{4,8},{8,4},{12,16},{16,12},{20,24},{24,20},{5,9},{9,5},{13,17},{1... | collective-permute-start | bytes 884744 | tf_op jit(solution)/shard_map/ppermute | solution.py:369
  9.7 17.6 %collective-permute-start.1 = (bf16[288,512]{1,0:T(8,128)(2,1)S(1)}, bf16[288,512]{1,0:T(8,128)(2,1)S(1)}, u32[]{:S(2)}, u32[]{:S(2)}) collective-permute-start(bf16[288,512]{1,0:T(8,128)(2,1)S(1)} %get-tuple-element.15.same_ref.sa_ref), channel_id=1, source_target_pairs={{0,4},{4,0},{8,12},{12,8},{16,20},{20,16},{24,28},{28,24},{1,5},{5... | collective-permute-start | bytes 884744 | tf_op jit(solution)/shard_map/ppermute | solution.py:369
  15.7 12.7 %copy-start.1 = (f32[4,512]{1,0:T(4,128)S(1)}, f32[4,512]{1,0:T(4,128)}, u32[]{:S(2)}) copy-start(f32[4,512]{1,0:T(4,128)} %gains_ref.3) | copy-start | bytes 24580
  24.5 15.3 %collective-permute-start.3 = (bf16[288,512]{1,0:T(8,128)(2,1)S(1)}, bf16[288,512]{1,0:T(8,128)(2,1)S(1)}, u32[]{:S(2)}, u32[]{:S(2)}) collective-permute-start(bf16[288,512]{1,0:T(8,128)(2,1)S(1)} %get-tuple-element.20.sb_ref), channel_id=1, source_target_pairs={{0,4},{4,0},{8,12},{12,8},{16,20},{20,16},{24,28},{28,24},{1,5},{5... | collective-permute-start | bytes 884744 | tf_op jit(solution)/shard_map/ppermute | solution.py:369
  24.6 15.3 %collective-permute-start.2 = (bf16[288,512]{1,0:T(8,128)(2,1)S(1)}, bf16[288,512]{1,0:T(8,128)(2,1)S(1)}, u32[]{:S(2)}, u32[]{:S(2)}) collective-permute-start(bf16[288,512]{1,0:T(8,128)(2,1)S(1)} %get-tuple-element.19.cb_ref), channel_id=1, source_target_pairs={{4,8},{8,4},{12,16},{16,12},{20,24},{24,20},{5,9},{9,5},{13,17},{1... | collective-permute-start | bytes 884744 | tf_op jit(solution)/shard_map/ppermute | solution.py:369
  27.3 12.5 %collective-permute-start.5 = (bf16[4,72,512]{2,1,0:T(8,128)(2,1)S(1)}, bf16[4,72,512]{2,1,0:T(8,128)(2,1)S(1)}, u32[]{:S(2)}, u32[]{:S(2)}) collective-permute-start(bf16[4,72,512]{2,1,0:T(8,128)(2,1)S(1)} %pad_maximum_fusion), channel_id=1, source_target_pairs={{1,0},{2,1},{3,2},{0,3},{5,4},{6,5},{7,6},{4,7},{9,8},{10,9},{11,1... | collective-permute-start | bytes 884744 | tf_op jit(solution)/shard_map/ppermute | solution.py:363
  28.4 11.4 %collective-permute-start.4 = (bf16[4,72,512]{2,1,0:T(8,128)(2,1)S(1)}, bf16[4,72,512]{2,1,0:T(8,128)(2,1)S(1)}, u32[]{:S(2)}, u32[]{:S(2)}) collective-permute-start(bf16[4,72,512]{2,1,0:T(8,128)(2,1)S(1)} %pad_maximum_fusion), channel_id=1, source_target_pairs={{3,0},{0,1},{1,2},{2,3},{7,4},{4,5},{5,6},{6,7},{11,8},{8,9},{9,10... | collective-permute-start | bytes 884744 | tf_op jit(solution)/shard_map/ppermute | solution.py:363
  28.4 11.4 %copy-start = (bf16[2,512,1536]{2,1,0:T(8,128)(2,1)S(1)}, bf16[2,512,1536]{2,1,0:T(8,128)(2,1)}, u32[]{:S(2)}) copy-start(bf16[2,512,1536]{2,1,0:T(8,128)(2,1)} %wqkv_ref.1) | copy-start | bytes 9437188
